TPU v7x, 256 devices: a whole 4x4x8 slice. The times are simulated.
256 devices in a mesh: image: 8 (over y, x_lo), slab: 32 (over x_hi, z, core).
Axes of the slice: x: 4 (x_hi: 2, x_lo: 2; x = x_hi * 2 + x_lo), y: 4, z: 8, core: 2. Of those that a mesh axis runs over, the one named last changes fastest.
Arguments:
- positions: float32 [16, 3, 8192], P('image', None, 'slab')
- neighbours: int32 [262144], P('slab'), may hold values from -1 to 511
- ghost_slots: int32 [2, 4096], P(None, 'slab'), may hold values from 0 to 255, as said below
- climbing: int32 [1], replicated, may hold values from 1 to 14
- w_radial1: float32 [8, 128], replicated, may hold values from -2 to 2
- w_square: float32 [128, 128], replicated, may hold values from -0.5 to 0.5
- w_hidden: float32 [128, 128], replicated, may hold values from -0.5 to 0.5
- w_message: float32 [128, 128], replicated, may hold values from -0.5 to 0.5
- w_radial2: float32 [8, 128], replicated, may hold values from -2 to 2
- w_output: float32 [128, 128], replicated, may hold values from -0.5 to 0.5
- w_energy: float32 [128], replicated, may hold values from -0.5 to 0.5
Outputs:
- neb_force: float32 [16, 3, 8192], P('image', None, 'slab')
- energies: float32 [16], P('image')
Inputs may be any that keep to these rules, and one draw needn't show every extreme that they name: `ghost_slots`: the two rows of one slab hold each of its atoms once.
All inputs are finite; a program needn't handle non-finite values.
Results may differ from a plain program's by a relative error of at most 0.0003.
Values sent between devices are 32-bit elements; how exact they have to be, the bound alone decides.
No kernel may reach another device: no remote copies, remote signals or barrier semaphores. Data moves between devices by JAX's collectives and lax.ppermute only.
A program may use at most 64 MiB of HBM per device.

v0:
```python
import math

import jax
import jax.numpy as jnp
from jax import lax
from jax.experimental import pallas as pl
from jax.experimental.pallas import tpu as pltpu
from jax.sharding import PartitionSpec as P

NB = 8
NX = 16
NY = 8
NZL = 2
LAYER = 128
CH = 128
NOFF = 26
ROWS = 40

LATTICE = 2.55
CUTOFF = 5.0
STIFFNESS = 5.0
F32 = jnp.float32
BF16 = jnp.bfloat16
I32 = jnp.int32

OFFSETS = [
    (dx, dy, dz)
    for dz in (-1, 0, 1)
    for dy in (-1, 0, 1)
    for dx in (-1, 0, 1)
    if (dx, dy, dz) != (0, 0, 0)
]
ROW_OF = {offset: row for row, offset in enumerate(OFFSETS)}
LATERALS = [(dx, dy) for dy in (-1, 0, 1) for dx in (-1, 0, 1)]
LATERAL_OF = {lateral: number for number, lateral in enumerate(LATERALS)}


def take(values, index):
    return jnp.take_along_axis(values, index, axis=1, mode="promise_in_bounds")


def iota(shape, dim):
    return lax.broadcasted_iota(I32, shape, dim)


def shifted_site(shape, dx, dy):
    lane = iota(shape, len(shape) - 1)
    return ((((lane >> 4) + dy) & (NY - 1)) << 4) | ((lane + dx) & (NX - 1))


def site_of_row():
    row = iota((32, LAYER), 0)
    code = row + (row >= 13).astype(I32)
    level = (code >= 9).astype(I32) + (code >= 18).astype(I32)
    rest = code - 9 * level
    line = (rest >= 3).astype(I32) + (rest >= 6).astype(I32)
    column = rest - 3 * line
    return shifted_site((32, LAYER), column - 1, line - 1) & (LAYER - 1)


def silu_parts(values):
    sigma = 1.0 / (1.0 + jnp.exp(-values))
    return values * sigma, sigma * (1.0 + values * (1.0 - sigma))


def halves(values):
    high = values.astype(BF16)
    low = (values - high.astype(F32)).astype(BF16)
    return high, low


def stationary(matrix):
    high, low = halves(matrix)
    return jnp.concatenate(
        [jnp.concatenate([high, high], axis=1), jnp.concatenate([low, low], axis=1)], axis=0
    )


def product(packed, values):
    high, low = halves(values)
    out = jnp.dot(packed, jnp.concatenate([high, low], axis=0), preferred_element_type=F32)
    rows = packed.shape[0] // 2
    return out[:rows] + out[rows:]


def radial_stationary(matrix):
    high, low = halves(matrix.T)
    return jnp.concatenate([high, high, low, low], axis=1)


def radial_moving(values):
    high = values.astype(BF16).astype(F32)
    both = jnp.concatenate([high, values - high], axis=0).astype(BF16)
    return jnp.concatenate([both, both], axis=0)


def prepare_kernel(positions, neighbours, ghost_slots, out, site_of_slot):
    slots = ghost_slots[...]
    inverse = jnp.zeros((8, 2 * LAYER), F32)
    for layer in range(NZL):
        hit = (jnp.broadcast_to(slots[layer : layer + 1], (2 * LAYER, LAYER)) == iota((2 * LAYER, LAYER), 0))
        sites = (iota((8, LAYER), 1) + layer * LAYER).astype(F32).astype(BF16)
        inverse = inverse + lax.dot_general(
            sites,
            jnp.where(hit, 1.0, 0.0).astype(BF16),
            (((1,), (1,)), ((), ())),
            preferred_element_type=F32,
        )
    inverse = inverse.astype(I32)
    site_of_slot[...] = inverse
    first = jnp.broadcast_to(inverse[0:1, :LAYER], (32, LAYER))
    second = jnp.broadcast_to(inverse[0:1, LAYER:], (32, LAYER))
    coords = jnp.concatenate([positions[0], positions[1], jnp.zeros((2, 2 * LAYER), F32)], axis=0)
    listed = neighbours[...].astype(F32)
    turned = jnp.concatenate([listed, jnp.zeros((64, LAYER), F32)], axis=0).T
    site = iota((32, LAYER), 1)
    row = iota((32, LAYER), 0)
    for layer in range(NZL):
        here = slice(layer * LAYER, (layer + 1) * LAYER)
        slot = jnp.broadcast_to(slots[layer : layer + 1], (8, LAYER))
        low = slot & (LAYER - 1)
        out[32:40, here] = jnp.where(slot < LAYER, take(coords[:, :LAYER], low), take(coords[:, LAYER:], low))
        slot = jnp.broadcast_to(slots[layer : layer + 1], (32, LAYER))
        picked = take(turned[0:32], slot >> 2)
        for part in range(1, 4):
            picked = jnp.where((slot & 3) == part, take(turned[32 * part : 32 * part + 32], slot >> 2), picked)
        entry = picked.astype(I32)
        low = entry & (LAYER - 1)
        own = jnp.where(entry < LAYER, take(first, low), take(second, low))
        inside = entry < 2 * LAYER
        level = jnp.where(inside, own >> 7, jnp.where(entry < 3 * LAYER, -1, NZL))
        target = jnp.where(inside, own & (LAYER - 1), low)
        column = ((target & (NX - 1)) - (site & (NX - 1)) + 1) & (NX - 1)
        line = ((target >> 4) - (site >> 4) + 1) & (NY - 1)
        code = (level - layer + 1) * 9 + line * 3 + column
        code = jnp.where(code > 13, code - 1, code) & 31
        bits = jnp.where(entry >= 0, jnp.left_shift(jnp.ones_like(code), code), 0)
        bits = bits[0:16] | bits[16:32]
        bits = bits[0:8] | bits[8:16]
        bits = bits[0:4] | bits[4:8]
        bits = bits[0:2] | bits[2:4]
        bits = bits[0:1] | bits[1:2]
        mask = (jnp.broadcast_to(bits, (32, LAYER)) >> row) & 1
        out[0:32, here] = jnp.where(row < NOFF, mask.astype(F32), 0.0)


SIN_TERMS = [(-1.0) ** k / math.factorial(2 * k + 1) for k in range(7)]
COS_TERMS = [(-1.0) ** k / math.factorial(2 * k) for k in range(8)]


def horner(terms, square):
    total = jnp.full_like(square, terms[-1])
    for term in terms[-2::-1]:
        total = total * square + term
    return total


def forces_kernel(
    cell_z,
    parity,
    below,
    middle,
    above,
    path,
    w_radial1,
    w_square,
    w_hidden,
    w_message,
    w_radial2,
    w_output,
    w_energy,
    kept,
    sent,
    sums,
    coords,
    reach,
    inverse_radius,
    phi,
    slope,
    summed,
    radial_mix,
    hidden,
    hidden_slope,
    message,
    edge_radial,
    grad_out,
    grad_summed,
    pair_grad,
    pair_grad_turned,
):
    even = parity[0] == 0
    blocks = [(ref, slice(k * LAYER, (k + 1) * LAYER)) for ref in (below, middle, above) for k in range(4)]
    for level, (ref, here) in enumerate(blocks):
        coords[level, 0:3] = jnp.where(even, ref[32:35, here], ref[35:38, here])
    row = iota((32, LAYER), 0)
    site = site_of_row()
    boxes = (NX * LATTICE, NY * LATTICE, cell_z)

    for e in range(10):
        ref, here = blocks[e + 1]
        mask = ref[0:32, here]
        squared = None
        for c in range(3):
            centre = coords[e + 1, c : c + 1]
            source = jnp.where(
                row < 9,
                jnp.broadcast_to(coords[e, c : c + 1], (32, LAYER)),
                jnp.where(
                    row < 17,
                    jnp.broadcast_to(centre, (32, LAYER)),
                    jnp.broadcast_to(coords[e + 2, c : c + 1], (32, LAYER)),
                ),
            )
            d = take(source, site) - jnp.broadcast_to(centre, (32, LAYER))
            box = jnp.float32(boxes[c])
            half = jnp.float32(0.5) * box
            d = jnp.where(d > half, d - box, jnp.where(d < -half, d + box, d))
            if 3 <= e <= 6:
                reach[e - 3, c] = d
            squared = d * d if squared is None else squared + d * d
        squared = jnp.where(squared > 0.0, squared, 1.0)
        radius = jnp.sqrt(squared)
        inverse = 1.0 / radius
        if 3 <= e <= 6:
            inverse_radius[e - 3] = inverse
        inside = radius < CUTOFF
        angle = jnp.minimum(radius * (math.pi / (2.0 * CUTOFF)), 0.5 * math.pi)
        square = angle * angle
        sine = angle * horner(SIN_TERMS, square)
        cosine = horner(COS_TERMS, square)
        sine1 = 2.0 * sine * cosine
        cosine1 = 1.0 - 2.0 * sine * sine
        smooth = jnp.where(inside, cosine * cosine, 0.0)
        cut_slope = jnp.where(inside, (-math.pi / CUTOFF) * sine * cosine, 0.0)
        scale = mask * smooth * inverse
        tilt = mask * (cut_slope - smooth * inverse) * inverse
        twice = 2.0 * cosine1
        s_prev, s_here = jnp.zeros_like(sine1), sine1
        c_prev, c_here = jnp.ones_like(sine1), cosine1
        for b in range(NB):
            phi[e, pl.ds(b, 32, stride=NB), :] = scale * s_here
            if 2 <= e <= 7:
                slope[e - 2, pl.ds(b, 32, stride=NB), :] = tilt * s_here + scale * (
                    ((b + 1) * math.pi / CUTOFF) * c_here
                )
            s_prev, s_here = s_here, twice * s_here - s_prev
            c_prev, c_here = c_here, twice * c_here - c_prev
        total = phi[e, 0:NB]
        for o in range(1, NOFF):
            total = total + phi[e, o * NB : (o + 1) * NB]
        summed[e] = total

    first = radial_stationary(w_radial1[...])
    second = radial_stationary(w_radial2[...])
    square_t = stationary(w_square[...].T)
    hidden_t = stationary(w_hidden[...].T)
    message_t = stationary(w_message[...].T)

    def nodes(pair, carry):
        e = 2 * pair
        mix = jnp.dot(
            first,
            radial_moving(jnp.concatenate([summed[e], summed[e + 1]], axis=1)),
            preferred_element_type=F32,
        )
        mixed = mix + product(square_t, mix * mix)
        act, act_slope = silu_parts(product(hidden_t, mixed))
        sent_on = product(message_t, act)
        for k in range(2):
            here = slice(k * LAYER, (k + 1) * LAYER)
            radial_mix[e + k] = mix[:, here]
            hidden[e + k] = act[:, here]
            hidden_slope[e + k] = act_slope[:, here]
            for number, (dx, dy) in enumerate(LATERALS):
                part = sent_on[:, here]
                if (dx, dy) != (0, 0):
                    part = take(part, shifted_site((CH, LAYER), dx, dy))
                message[number, e + k] = part
        return carry

    lax.fori_loop(0, 5, nodes, 0)

    output_t = stationary(w_output[...].T)
    output_n = stationary(w_output[...])
    weight = jnp.broadcast_to(w_energy[...], (8, CH)).T[:, 0:1]

    def readout(pair, energy):
        a = 2 * pair
        e = a + 1
        total = jnp.concatenate([hidden[e], hidden[e + 1]], axis=1)
        for o, (dx, dy, dz) in enumerate(OFFSETS):
            here = slice(o * NB, (o + 1) * NB)
            radial = jnp.dot(
                second,
                radial_moving(jnp.concatenate([phi[e, here], phi[e + 1, here]], axis=1)),
                preferred_element_type=F32,
            )
            edge_radial[a, o] = radial[:, :LAYER]
            edge_radial[a + 1, o] = radial[:, LAYER:]
            number = LATERAL_OF[(dx, dy)]
            total = total + radial * jnp.concatenate([message[number, e + dz], message[number, e + 1 + dz]], axis=1)
        act, act_slope = silu_parts(product(output_t, total))
        grad = product(output_n, weight * act_slope)
        grad_out[a] = grad[:, :LAYER]
        grad_out[a + 1] = grad[:, LAYER:]
        part = jnp.sum(weight * act, axis=0, keepdims=True)
        own = jnp.logical_or(pair == 1, pair == 2)
        return energy + jnp.where(own, part, 0.0)

    energy = lax.fori_loop(0, 4, readout, jnp.zeros((1, 2 * LAYER), F32))

    message_n = stationary(w_message[...])
    hidden_n = stationary(w_hidden[...])
    square_n = stationary(w_square[...])
    first_n = stationary(w_radial1[...])
    second_n = stationary(w_radial2[...])

    def back(pair, carry):
        f = 2 * pair
        parts = []
        for k in range(2):
            grad_message = None
            for dx, dy in LATERALS:
                total = None
                for dz in (-1, 0, 1):
                    if (dx, dy, dz) == (0, 0, 0):
                        continue
                    a = f + k + 1 - dz
                    term = grad_out[a] * edge_radial[a, ROW_OF[(dx, dy, dz)]]
                    total = term if total is None else total + term
                if (dx, dy) != (0, 0):
                    total = take(total, shifted_site((CH, LAYER), -dx, -dy))
                grad_message = total if grad_message is None else grad_message + total
            parts.append(grad_message)
        grad_hidden = jnp.concatenate([grad_out[f + 1], grad_out[f + 2]], axis=1) + product(
            message_n, jnp.concatenate(parts, axis=1)
        )
        grad_pre = grad_hidden * jnp.concatenate([hidden_slope[f + 2], hidden_slope[f + 3]], axis=1)
        grad_mixed = product(hidden_n, grad_pre)
        mix = jnp.concatenate([radial_mix[f + 2], radial_mix[f + 3]], axis=1)
        grad_radial = grad_mixed + 2.0 * mix * product(square_n, grad_mixed)
        grad = product(first_n, grad_radial)
        grad_summed[f] = grad[:, :LAYER]
        grad_summed[f + 1] = grad[:, LAYER:]
        return carry

    lax.fori_loop(0, 3, back, 0)

    for f in range(6):
        pair_grad_turned[f] = jnp.zeros((32, LAYER), F32)
    for f in range(4):
        pair_grad[f] = jnp.zeros((32, LAYER), F32)

    def edges(f0, f1, offset0, offset1):
        number = LATERAL_OF[offset0[:2]]
        moved = jnp.concatenate(
            [
                grad_out[f0 + 1] * message[number, f0 + 2 + offset0[2]],
                grad_out[f1 + 1] * message[number, f1 + 2 + offset1[2]],
            ],
            axis=1,
        )
        grad = product(second_n, moved)
        out = []
        for k, (f, offset) in enumerate(((f0, offset0), (f1, offset1))):
            o = ROW_OF[offset]
            value = (grad[:, k * LAYER : (k + 1) * LAYER] + grad_summed[f]) * slope[f, o * NB : (o + 1) * NB]
            out.append(jnp.sum(value, axis=0, keepdims=True))
        return out

    def own_edges(pair, carry):
        f = 2 * pair + 1
        for o, offset in enumerate(OFFSETS):
            left, right = edges(f, f + 1, offset, offset)
            pair_grad[f - 1, o : o + 1] = left
            pair_grad[f, o : o + 1] = right
            pair_grad_turned[f, 25 - o : 26 - o] = left
            pair_grad_turned[f + 1, 25 - o : 26 - o] = right
        return carry

    lax.fori_loop(0, 2, own_edges, 0)
    for dx, dy in LATERALS:
        up, down = (dx, dy, 1), (dx, dy, -1)
        left, right = edges(0, 5, up, down)
        pair_grad_turned[0, 25 - ROW_OF[up] : 26 - ROW_OF[up]] = left
        pair_grad_turned[5, 25 - ROW_OF[down] : 26 - ROW_OF[down]] = right

    force_parts = []
    for f in range(1, 5):
        source = jnp.where(
            row < 9, pair_grad_turned[f - 1], jnp.where(row < 17, pair_grad_turned[f], pair_grad_turned[f + 1])
        )
        pull = (pair_grad[f - 1] + take(source, site)) * inverse_radius[f - 1]
        force_parts.append(
            jnp.concatenate([jnp.sum(pull * reach[f - 1, c], axis=0, keepdims=True) for c in range(3)], axis=0)
        )
    force = jnp.concatenate(force_parts, axis=1)

    low, high = middle[32:35, :], middle[35:38, :]
    beside = path[0:3, :]
    up = jnp.where(even, high - low, beside - high)
    down = jnp.where(even, low - beside, high - low)
    lane = iota((1, LAYER), 1)
    values = jnp.zeros((1, LAYER), F32)
    terms = (
        energy,
        force * up,
        force * down,
        up * up,
        down * down,
        up * down,
    )
    for k, term in enumerate(terms):
        values = values + jnp.where(lane == k, jnp.sum(term), 0.0)
    sums[...] = values
    both = jnp.concatenate([force, beside, jnp.zeros((2, 4 * LAYER), F32)], axis=0)
    left, right = both[:, : 2 * LAYER], both[:, 2 * LAYER :]
    kept[...] = jnp.where(even, left, right)
    sent[...] = jnp.where(even, right, left)


def combine_kernel(image_group, parity, climbing, table, own, kept, received, site_of_slot, out, energies, totals):
    even = parity[0] == 0
    group = image_group[0]
    groups = table.shape[0] // 32
    for g in range(groups):
        total = table[32 * g : 32 * g + 8]
        for k in range(1, 4):
            total = total + table[32 * g + 8 * k : 32 * g + 8 * k + 8]
        total = total[0:4] + total[4:8]
        totals[2 * g : 2 * g + 2] = total[0:2] + total[2:4]
    images = 2 * groups
    low, high = own[32:35, :], own[35:38, :]
    f_kept, f_received = kept[0:3, :], received[0:3, :]
    p_kept, p_received = kept[3:6, :], received[3:6, :]
    sides = (
        (jnp.where(even, f_kept, f_received), high - low, low - jnp.where(even, p_kept, p_received)),
        (jnp.where(even, f_received, f_kept), jnp.where(even, p_received, p_kept) - high, high - low),
    )
    slot = jnp.concatenate([site_of_slot[...]], axis=0)
    for k, (force, up, down) in enumerate(sides):
        image = 2 * group + k
        here = totals[pl.ds(image, 1), :]
        after = totals[pl.ds(jnp.minimum(image + 1, images - 1), 1), :]
        before = totals[pl.ds(jnp.maximum(image - 1, 0), 1), :]
        v_here, v_next, v_prev = here[:, 0:1], after[:, 0:1], before[:, 0:1]
        big = jnp.maximum(jnp.abs(v_next - v_here), jnp.abs(v_prev - v_here))
        small = jnp.minimum(jnp.abs(v_next - v_here), jnp.abs(v_prev - v_here))
        rising = jnp.logical_and(v_next > v_here, v_here > v_prev)
        falling = jnp.logical_and(v_next < v_here, v_here < v_prev)
        higher = v_next > v_prev
        a = jnp.where(rising, 1.0, jnp.where(falling, 0.0, jnp.where(higher, big, small)))
        b = jnp.where(rising, 0.0, jnp.where(falling, 1.0, jnp.where(higher, small, big)))
        fu, fd, uu, dd, ud = (here[:, i : i + 1] for i in range(1, 6))
        tangent_sq = a * a * uu + 2.0 * a * b * ud + b * b * dd
        norm = jnp.sqrt(tangent_sq)
        along = (a * fu + b * fd) / norm
        pull = STIFFNESS * (jnp.sqrt(uu) - jnp.sqrt(dd))
        amount = jnp.where(image == climbing[0], 2.0 * along, along - pull) / norm
        tangent = a * up + b * down
        result = force - amount * tangent
        end = jnp.logical_or(image == 0, image == images - 1)
        result = jnp.where(end, 0.0, result)
        result = jnp.concatenate([result, jnp.zeros((5, 2 * LAYER), F32)], axis=0)
        for part in range(NZL):
            index = slot[:, part * LAYER : (part + 1) * LAYER]
            low_index = index & (LAYER - 1)
            back = jnp.where(index < LAYER, take(result[:, :LAYER], low_index), take(result[:, LAYER:], low_index))
            out[k, :, part * LAYER : (part + 1) * LAYER] = back[0:3]
        energies[k] = here[0, 0]


def vmem():
    return pl.BlockSpec(memory_space=pltpu.VMEM)


def smem():
    return pl.BlockSpec(memory_space=pltpu.SMEM)


def local(
    positions,
    neighbours,
    ghost_slots,
    climbing,
    w_radial1,
    w_square,
    w_hidden,
    w_message,
    w_radial2,
    w_output,
    w_energy,
):
    slabs = lax.axis_size("slab")
    groups = lax.axis_size("image")
    group = lax.axis_index("image")
    slab = lax.axis_index("slab")
    parity = slab % 2
    even = parity == 0
    parity_arg = parity.astype(I32).reshape(1)

    prepared, site_of_slot = pl.pallas_call(
        prepare_kernel,
        out_shape=(
            jax.ShapeDtypeStruct((ROWS, 2 * LAYER), F32),
            jax.ShapeDtypeStruct((8, 2 * LAYER), I32),
        ),
        in_specs=[vmem()] * 3,
        out_specs=(vmem(), vmem()),
    )(positions, neighbours.reshape(64, LAYER), ghost_slots)

    mate = lax.ppermute(prepared, "slab", [(i, i ^ 1) for i in range(slabs)])
    middle = jnp.concatenate([jnp.where(even, prepared, mate), jnp.where(even, mate, prepared)], axis=1)
    below = lax.ppermute(middle, "slab", [(i, (i + 2) % slabs) for i in range(slabs)])
    above = lax.ppermute(middle, "slab", [((i + 2) % slabs, i) for i in range(slabs)])
    mine = jnp.where(even, middle[32:35], middle[35:38])
    hops = []
    for g in range(groups):
        for s in range(slabs):
            if s % 2 and g + 1 < groups:
                hops.append((g * slabs + s, (g + 1) * slabs + s - 1))
            if s % 2 == 0 and g > 0:
                hops.append((g * slabs + s, (g - 1) * slabs + s + 1))
    path = lax.ppermute(mine, ("image", "slab"), hops)

    kept, sent, sums = pl.pallas_call(
        lambda *refs: forces_kernel(slabs * NZL * LATTICE, *refs),
        out_shape=(
            jax.ShapeDtypeStruct((8, 2 * LAYER), F32),
            jax.ShapeDtypeStruct((8, 2 * LAYER), F32),
            jax.ShapeDtypeStruct((1, LAYER), F32),
        ),
        in_specs=[smem()] + [vmem()] * 11,
        out_specs=(vmem(), vmem(), vmem()),
        scratch_shapes=[
            pltpu.VMEM((12, 8, LAYER), F32),
            pltpu.VMEM((4, 3, 32, LAYER), F32),
            pltpu.VMEM((4, 32, LAYER), F32),
            pltpu.VMEM((10, 32 * NB, LAYER), F32),
            pltpu.VMEM((6, 32 * NB, LAYER), F32),
            pltpu.VMEM((10, NB, LAYER), F32),
            pltpu.VMEM((10, CH, LAYER), F32),
            pltpu.VMEM((10, CH, LAYER), F32),
            pltpu.VMEM((10, CH, LAYER), F32),
            pltpu.VMEM((9, 10, CH, LAYER), F32),
            pltpu.VMEM((8, NOFF, CH, LAYER), F32),
            pltpu.VMEM((8, CH, LAYER), F32),
            pltpu.VMEM((6, NB, LAYER), F32),
            pltpu.VMEM((4, 32, LAYER), F32),
            pltpu.VMEM((6, 32, LAYER), F32),
        ],
        compiler_params=pltpu.CompilerParams(vmem_limit_bytes=48 * 1024 * 1024),
    )(
        parity_arg,
        below,
        middle,
        above,
        path,
        w_radial1,
        w_square,
        w_hidden,
        w_message,
        w_radial2,
        w_output,
        w_energy.reshape(1, CH),
    )

    devices = groups * slabs
    received = lax.ppermute(sent, "slab", [(i, i ^ 1) for i in range(slabs)])
    table = lax.all_to_all(
        jnp.broadcast_to(sums[None], (devices, 1, LAYER)), ("image", "slab"), 0, 0, tiled=False
    ).reshape(devices, LAYER)

    return pl.pallas_call(
        combine_kernel,
        out_shape=(
            jax.ShapeDtypeStruct(positions.shape, F32),
            jax.ShapeDtypeStruct((2,), F32),
        ),
        in_specs=[smem()] * 3 + [vmem()] * 5,
        out_specs=(vmem(), smem()),
        scratch_shapes=[pltpu.VMEM((2 * groups, LAYER), F32)],
    )(
        group.astype(I32).reshape(1),
        parity_arg,
        climbing,
        table,
        prepared,
        kept,
        received,
        site_of_slot,
    )


def solution(mesh):
    return jax.shard_map(
        local,
        mesh=mesh,
        in_specs=(
            P("image", None, "slab"),
            P("slab"),
            P(None, "slab"),
            P(),
            P(),
            P(),
            P(),
            P(),
            P(),
            P(),
            P(),
        ),
        out_specs=(P("image", None, "slab"), P("image")),
        check_vma=False,
    )
```

profile of v0, /device:TPU:1, one launch (start us, length us, event | category | flops | bytes accessed | tf_op | source)
XLA Modules:
  0.0 67.8 jit_solution(11176728084356156698)
XLA Ops:
  0.6 1.3 %copy.15.positions = f32[2,3,256]{2,1,0:T(4,128)} copy(f32[2,3,256]{2,0,1:T(2,128)} %param.11) | data formatting | bytes 12288 | tf_op args[0]
  1.9 1.8 %shard_map.122 = (f32[40,256]{1,0:T(8,128)}, s32[8,256]{1,0:T(8,128)}) custom-call(f32[2,3,256]{2,1,0:T(4,128)} %copy.15.positions, s32[64,128]{1,0:T(8,128)} %bitcast.9, s32[2,128]{1,0:T(2,128)} %ghost_slots.1), custom_call_target="tpu_custom_call" | custom-call | tf_op jit(solution)/shard_map/pallas_call | solution.py:502
  3.7 3.2 %collective-permute-start = (f32[40,256]{1,0:T(8,128)}, f32[40,256]{1,0:T(8,128)S(1)}, u32[]{:S(2)}, u32[]{:S(2)}) collective-permute-start(f32[40,256]{1,0:T(8,128)} %get-tuple-element.7.own), channel_id=1, source_target_pairs={{0,1},{1,0},{2,3},{3,2},{4,5},{5,4},{6,7},{7,6},{8,9},{9,8},{10,11... | collective-permute-start | bytes 122888 | tf_op jit(solution)/shard_map/ppermute | solution.py:512
  6.9 1.1 %collective-permute-done = f32[40,256]{1,0:T(8,128)S(1)} collective-permute-done((f32[40,256]{1,0:T(8,128)}, f32[40,256]{1,0:T(8,128)S(1)}, u32[]{:S(2)}, u32[]{:S(2)}) %collective-permute-start) | collective-permute-done | bytes 40992 | tf_op jit(solution)/shard_map/ppermute | solution.py:512
  8.0 0.8 %broadcast_select_fusion.1 = (f32[40,256]{1,0:T(8,128)S(1)}, f32[40,256]{1,0:T(8,128)S(1)}) fusion(f32[40,256]{1,0:T(8,128)} %get-tuple-element.7.own, f32[40,256]{1,0:T(8,128)S(1)} %collective-permute-done, pred[]{:T(512)S(6)} %eq.5), kind=kLoop, calls=%fused_computation.6 | loop fusion | flops 20480 | bytes 163841 | tf_op jit(solution)/shard_map/jit(_where)/select_n | solution.py:513
  8.8 0.0 copy-start.2
  8.9 0.0 copy-start
  8.9 0.1 collective-permute-start.1
  9.0 6.4 %collective-permute-start.2 = (f32[40,512]{1,0:T(8,128)S(1)}, f32[40,512]{1,0:T(8,128)S(1)}, u32[]{:S(2)}, u32[]{:S(2)}) collective-permute-start(f32[40,512]{1,0:T(8,128)S(1)} %pad_maximum_fusion.refs_2_), channel_id=1, source_target_pairs={{2,0},{3,1},{4,2},{5,3},{6,4},{7,5},{8,6},{9,7},{10,8},{11,9},{12,... | collective-permute-start | bytes 245768 | tf_op jit(solution)/shard_map/ppermute | solution.py:515
  15.3 2.9 %collective-permute-start.3 = (f32[3,512]{1,0:T(4,128)S(1)}, f32[3,512]{1,0:T(4,128)S(1)}, u32[]{:S(2)}, u32[]{:S(2)}) collective-permute-start(f32[3,512]{1,0:T(4,128)S(1)} %fusion.1), channel_id=1, source_target_pairs={{1,32},{3,34},{5,36},{7,38},{9,40},{11,42},{13,44},{15,46},{17,48}... | collective-permute-start | bytes 18440 | tf_op jit(solution)/shard_map/ppermute | solution.py:524
  18.2 2.2 %collective-permute-done.3.refs_4_ = f32[3,512]{1,0:T(4,128)S(1)} collective-permute-done((f32[3,512]{1,0:T(4,128)S(1)}, f32[3,512]{1,0:T(4,128)S(1)}, u32[]{:S(2)}, u32[]{:S(2)}) %collective-permute-start.3) | collective-permute-done | bytes 6176 | tf_op jit(solution)/shard_map/ppermute | solution.py:524
  20.4 0.0 collective-permute-done.1.refs_1_
  20.5 0.0 collective-permute-done.2.refs_3_
  20.5 0.6 copy-done.7
  21.1 18.2 %shard_map.123 = (f32[8,256]{1,0:T(8,128)S(1)}, f32[8,256]{1,0:T(8,128)S(1)}, f32[1,128]{1,0:T(1,128)S(1)}) custom-call(s32[1]{0:T(128)} %bitcast.1.refs_0_.parity, f32[40,512]{1,0:T(8,128)S(1)} %collective-permute-done.1.refs_1_, f32[40,512]{1,0:T(8,128)S(1)} %pad_maximum_fusion.refs_2_, f32[40,512]{1,0:T(8,128)S(1)} %collective-permute-done.2.refs_3_, ...), custom_call_target="tpu_custom_call" | custom-call | tf_op jit(solution)/shard_map/pallas_call | solution.py:526
  39.4 0.6 copy-done.4
  40.0 0.7 %broadcast_in_dim.9 = f32[256,1,128]{2,1,0:T(1,128)} broadcast(f32[128]{0:T(128)S(1)} %bitcast.6), dimensions={2} | broadcast | bytes 131584 | tf_op jit(solution)/shard_map/broadcast_in_dim | solution.py:571
  40.7 10.5 %all-to-all-start = ((f32[256,1,128]{2,1,0:T(1,128)}), f32[256,1,128]{2,1,0:T(1,128)S(1)}, u32[]{:S(2)}, u32[]{:S(2)}) async-start(f32[256,1,128]{2,1,0:T(1,128)} %broadcast_in_dim.9), calls=%async_computation | async-start | bytes 262144 | tf_op jit(solution)/shard_map/all_to_all | solution.py:570
  51.2 2.2 %collective-permute-start.4 = (f32[8,256]{1,0:T(8,128)S(1)}, f32[8,256]{1,0:T(8,128)S(1)}, u32[]{:S(2)}, u32[]{:S(2)}) collective-permute-start(f32[8,256]{1,0:T(8,128)S(1)} %get-tuple-element.10), channel_id=1, source_target_pairs={{0,1},{1,0},{2,3},{3,2},{4,5},{5,4},{6,7},{7,6},{8,9},{9,8},{10,11... | collective-permute-start | bytes 24584 | tf_op jit(solution)/shard_map/ppermute | solution.py:569
  54.1 0.2 collective-permute-done.4.received
  54.3 9.8 %all-to-all-done = f32[256,1,128]{2,1,0:T(1,128)S(1)} async-done(((f32[256,1,128]{2,1,0:T(1,128)}), f32[256,1,128]{2,1,0:T(1,128)S(1)}, u32[]{:S(2)}, u32[]{:S(2)}) %all-to-all-start) | async-done | bytes 131104 | tf_op jit(solution)/shard_map/all_to_all | solution.py:570
  64.1 0.6 copy-done.8
  64.7 1.8 %shard_map.124 = (f32[2,3,256]{2,1,0:T(4,128)}, f32[2]{0:T(128)}) custom-call(s32[1]{0:T(128)} %bitcast.image_group, s32[1]{0:T(128)} %bitcast.1.refs_0_.parity, s32[1]{0:T(128)S(6)} %copy.17.climbing, f32[256,128]{1,0:T(8,128)} %bitcast.8, f32[40,256]{1,0:T(8,128)} %get-tuple-element.7.own, f32[8,256]{1,0:T(8,128)} %copy-done.4, f32[8,256]{1,0:T(8,128)} %copy-done.9, ...), custom_call_target="tpu_custom_call" | custom-call | tf_op jit(solution)/shard_map/pallas_call | solution.py:574
  66.5 1.3 %copy.16 = f32[2,3,256]{2,0,1:T(2,128)} copy(f32[2,3,256]{2,1,0:T(4,128)} %get-tuple-element.14) | data formatting | bytes 12288 | tf_op jit(solution)/shard_map/pallas_call | solution.py:574
  (17 shorter events, 0.0 us)
Async XLA Ops:
  3.7 4.3 %collective-permute-start = (f32[40,256]{1,0:T(8,128)}, f32[40,256]{1,0:T(8,128)S(1)}, u32[]{:S(2)}, u32[]{:S(2)}) collective-permute-start(f32[40,256]{1,0:T(8,128)} %get-tuple-element.7.own), channel_id=1, source_target_pairs={{0,1},{1,0},{2,3},{3,2},{4,5},{5,4},{6,7},{7,6},{8,9},{9,8},{10,11... | collective-permute-start | bytes 122888 | tf_op jit(solution)/shard_map/ppermute | solution.py:512
  8.0 12.5 %copy-start.3 = (f32[128,128]{1,0:T(8,128)S(1)}, f32[128,128]{1,0:T(8,128)}, u32[]{:S(2)}) copy-start(f32[128,128]{1,0:T(8,128)} %refs_10_.1) | copy-start | bytes 196612
  8.8 11.6 %copy-start.1 = (f32[128,128]{1,0:T(8,128)S(1)}, f32[128,128]{1,0:T(8,128)}, u32[]{:S(2)}) copy-start(f32[128,128]{1,0:T(8,128)} %refs_7_.1) | copy-start | bytes 196612
  8.8 11.7 %copy-start.2 = (f32[128,128]{1,0:T(8,128)S(1)}, f32[128,128]{1,0:T(8,128)}, u32[]{:S(2)}) copy-start(f32[128,128]{1,0:T(8,128)} %refs_8_.1) | copy-start | bytes 196612
  8.9 11.6 %copy-start = (f32[128,128]{1,0:T(8,128)S(1)}, f32[128,128]{1,0:T(8,128)}, u32[]{:S(2)}) copy-start(f32[128,128]{1,0:T(8,128)} %refs_6_.1) | copy-start | bytes 196612
  8.9 11.6 %collective-permute-start.1 = (f32[40,512]{1,0:T(8,128)S(1)}, f32[40,512]{1,0:T(8,128)S(1)}, u32[]{:S(2)}, u32[]{:S(2)}) collective-permute-start(f32[40,512]{1,0:T(8,128)S(1)} %pad_maximum_fusion.refs_2_), channel_id=1, source_target_pairs={{0,2},{1,3},{2,4},{3,5},{4,6},{5,7},{6,8},{7,9},{8,10},{9,11},{10,... | collective-permute-start | bytes 245768 | tf_op jit(solution)/shard_map/ppermute | solution.py:514
  9.0 11.5 %collective-permute-start.2 = (f32[40,512]{1,0:T(8,128)S(1)}, f32[40,512]{1,0:T(8,128)S(1)}, u32[]{:S(2)}, u32[]{:S(2)}) collective-permute-start(f32[40,512]{1,0:T(8,128)S(1)} %pad_maximum_fusion.refs_2_), channel_id=1, source_target_pairs={{2,0},{3,1},{4,2},{5,3},{6,4},{7,5},{8,6},{9,7},{10,8},{11,9},{12,... | collective-permute-start | bytes 245768 | tf_op jit(solution)/shard_map/ppermute | solution.py:515
  15.3 5.2 %copy-start.5 = (f32[8,128]{1,0:T(8,128)S(1)}, f32[8,128]{1,0:T(8,128)}, u32[]{:S(2)}) copy-start(f32[8,128]{1,0:T(8,128)} %refs_5_.1) | copy-start | bytes 12292
  15.3 5.2 %copy-start.6 = (f32[8,128]{1,0:T(8,128)S(1)}, f32[8,128]{1,0:T(8,128)}, u32[]{:S(2)}) copy-start(f32[8,128]{1,0:T(8,128)} %refs_9_.1) | copy-start | bytes 12292
  15.3 5.1 %collective-permute-start.3 = (f32[3,512]{1,0:T(4,128)S(1)}, f32[3,512]{1,0:T(4,128)S(1)}, u32[]{:S(2)}, u32[]{:S(2)}) collective-permute-start(f32[3,512]{1,0:T(4,128)S(1)} %fusion.1), channel_id=1, source_target_pairs={{1,32},{3,34},{5,36},{7,38},{9,40},{11,42},{13,44},{15,46},{17,48}... | collective-permute-start | bytes 18440 | tf_op jit(solution)/shard_map/ppermute | solution.py:524
  20.5 0.7 copy-start.7
  39.4 0.6 copy-start.4
  40.7 23.4 %all-to-all-start = ((f32[256,1,128]{2,1,0:T(1,128)}), f32[256,1,128]{2,1,0:T(1,128)S(1)}, u32[]{:S(2)}, u32[]{:S(2)}) async-start(f32[256,1,128]{2,1,0:T(1,128)} %broadcast_in_dim.9), calls=%async_computation | async-start | bytes 262144 | tf_op jit(solution)/shard_map/all_to_all | solution.py:570
  51.2 3.1 %collective-permute-start.4 = (f32[8,256]{1,0:T(8,128)S(1)}, f32[8,256]{1,0:T(8,128)S(1)}, u32[]{:S(2)}, u32[]{:S(2)}) collective-permute-start(f32[8,256]{1,0:T(8,128)S(1)} %get-tuple-element.10), channel_id=1, source_target_pairs={{0,1},{1,0},{2,3},{3,2},{4,5},{5,4},{6,7},{7,6},{8,9},{9,8},{10,11... | collective-permute-start | bytes 24584 | tf_op jit(solution)/shard_map/ppermute | solution.py:569
  54.3 9.8 %copy-start.9 = (f32[8,256]{1,0:T(8,128)}, f32[8,256]{1,0:T(8,128)S(1)}, u32[]{:S(2)}) copy-start(f32[8,256]{1,0:T(8,128)S(1)} %collective-permute-done.4.received) | copy-start | bytes 24580
  64.1 0.6 copy-start.8
where the time goes:
time: 68.2 us; the launch traced here: 67.8 us
  starting transfers between devices  25.3 us (37%)
  Pallas kernels  21.8 us (32%)
  waiting for transfers between devices  13.3 us (20%)
  local copies, waits for them, and re-layouts  5.16 us (8%)
  between operations  1.42 us (2%)
  other arithmetic  0.83 us (1%)
    pallas_call x1, Pallas kernels, local(): pl.pallas_call(lambda *refs: forces_kernel(slabs * NZL * LATTICE, *refs),...  18.2 us
    all_to_all x1, starting transfers between devices, local(): lax.all_to_all(jnp.broadcast_to(sums[None], (devices, 1, LAYER)), ('image...  10.5 us
    all_to_all x1, waiting for transfers between devices, local(): lax.all_to_all(jnp.broadcast_to(sums[None], (devices, 1, LAYER)), ('image...  9.8 us
    ppermute x1, starting transfers between devices, local(): lax.ppermute(middle, 'slab', [((i + 2) % slabs, i) for i in range(slabs)])  6.38 us
    ppermute x1, starting transfers between devices, local(): mate = lax.ppermute(prepared, 'slab', [(i, i ^ 1) for i in range(slabs)])  3.24 us
    unnamed x21, local copies, waits for them, and re-layouts  3.15 us
    ppermute x1, starting transfers between devices, local(): path = lax.ppermute(mine, ('image', 'slab'), hops)  2.87 us
    ppermute x1, starting transfers between devices, local(): received = lax.ppermute(sent, 'slab', [(i, i ^ 1) for i in range(slabs)])  2.23 us
  transfers between devices with their start and end apart: 6, of which 4 were waited for; matrix products, arithmetic and copies ran while one was open for 0% of the time, Pallas kernels for 0%

commit v1 on v0

--- a/solution.py
+++ b/solution.py
@@ -94,8 +94,8 @@
     return jnp.concatenate([both, both], axis=0)
 
 
-def prepare_kernel(positions, neighbours, ghost_slots, out, site_of_slot):
-    slots = ghost_slots[...]
+def prepare_kernel(packed, out, site_of_slot):
+    slots = packed[64:66, :].astype(I32)
     inverse = jnp.zeros((8, 2 * LAYER), F32)
     for layer in range(NZL):
         hit = (jnp.broadcast_to(slots[layer : layer + 1], (2 * LAYER, LAYER)) == iota((2 * LAYER, LAYER), 0))
@@ -110,8 +110,15 @@
     site_of_slot[...] = inverse
     first = jnp.broadcast_to(inverse[0:1, :LAYER], (32, LAYER))
     second = jnp.broadcast_to(inverse[0:1, LAYER:], (32, LAYER))
-    coords = jnp.concatenate([positions[0], positions[1], jnp.zeros((2, 2 * LAYER), F32)], axis=0)
-    listed = neighbours[...].astype(F32)
+    sides = [
+        jnp.concatenate(
+            [packed[66 + 4 * c + 2 * half + k : 67 + 4 * c + 2 * half + k] for k in range(2) for c in range(3)]
+            + [jnp.zeros((2, LAYER), F32)],
+            axis=0,
+        )
+        for half in range(2)
+    ]
+    listed = packed[0:64, :]
     turned = jnp.concatenate([listed, jnp.zeros((64, LAYER), F32)], axis=0).T
     site = iota((32, LAYER), 1)
     row = iota((32, LAYER), 0)
@@ -119,7 +126,7 @@
         here = slice(layer * LAYER, (layer + 1) * LAYER)
         slot = jnp.broadcast_to(slots[layer : layer + 1], (8, LAYER))
         low = slot & (LAYER - 1)
-        out[32:40, here] = jnp.where(slot < LAYER, take(coords[:, :LAYER], low), take(coords[:, LAYER:], low))
+        out[32:40, here] = jnp.where(slot < LAYER, take(sides[0], low), take(sides[1], low))
         slot = jnp.broadcast_to(slots[layer : layer + 1], (32, LAYER))
         picked = take(turned[0:32], slot >> 2)
         for part in range(1, 4):
@@ -155,38 +162,49 @@
     return total
 
 
-def forces_kernel(
+SQUARE, HIDDEN, MESSAGE, OUTPUT = range(4)
+
+
+def weights_kernel(squares, radials, turned, straight, radial, radial_turned, energy):
+    for number in range(4):
+        turned[number] = stationary(squares[number].T)
+        straight[number] = stationary(squares[number])
+    for number in range(2):
+        radial[number] = stationary(radials[number])
+        radial_turned[number] = radial_stationary(radials[number])
+    energy[...] = jnp.broadcast_to(radials[2, 0:1], (CH, CH)).T
+
+
+def stacked(arrays):
+    shape = (len(arrays),) + arrays[0].shape
+    out = jnp.broadcast_to(arrays[-1][None], shape)
+    for number, array in enumerate(arrays[:-1]):
+        out = jnp.where(iota(shape, 0) == number, jnp.broadcast_to(array[None], shape), out)
+    return out
+
+
+def forward_kernel(
     cell_z,
     parity,
     below,
     middle,
     above,
-    path,
-    w_radial1,
-    w_square,
-    w_hidden,
-    w_message,
-    w_radial2,
-    w_output,
+    turned,
+    straight,
+    radial_turned,
     w_energy,
-    kept,
-    sent,
-    sums,
-    coords,
+    along,
     reach,
     inverse_radius,
-    phi,
     slope,
-    summed,
     radial_mix,
-    hidden,
     hidden_slope,
     message,
-    edge_radial,
+    phi,
     grad_out,
-    grad_summed,
-    pair_grad,
-    pair_grad_turned,
+    coords,
+    summed,
+    hidden,
 ):
     even = parity[0] == 0
     blocks = [(ref, slice(k * LAYER, (k + 1) * LAYER)) for ref in (below, middle, above) for k in range(4)]
@@ -250,13 +268,10 @@
             total = total + phi[e, o * NB : (o + 1) * NB]
         summed[e] = total
 
-    first = radial_stationary(w_radial1[...])
-    second = radial_stationary(w_radial2[...])
-    square_t = stationary(w_square[...].T)
-    hidden_t = stationary(w_hidden[...].T)
-    message_t = stationary(w_message[...].T)
-
-    def nodes(pair, carry):
+    first, second = radial_turned[0], radial_turned[1]
+    square_t, hidden_t, message_t = turned[SQUARE], turned[HIDDEN], turned[MESSAGE]
+
+    def nodes(pair):
         e = 2 * pair
         mix = jnp.dot(
             first,
@@ -268,23 +283,23 @@
         sent_on = product(message_t, act)
         for k in range(2):
             here = slice(k * LAYER, (k + 1) * LAYER)
-            radial_mix[e + k] = mix[:, here]
             hidden[e + k] = act[:, here]
-            hidden_slope[e + k] = act_slope[:, here]
+            if 2 <= e <= 6:
+                radial_mix[e + k - 2] = mix[:, here]
+                hidden_slope[e + k - 2] = act_slope[:, here]
             for number, (dx, dy) in enumerate(LATERALS):
                 part = sent_on[:, here]
                 if (dx, dy) != (0, 0):
                     part = take(part, shifted_site((CH, LAYER), dx, dy))
                 message[number, e + k] = part
-        return carry
-
-    lax.fori_loop(0, 5, nodes, 0)
-
-    output_t = stationary(w_output[...].T)
-    output_n = stationary(w_output[...])
-    weight = jnp.broadcast_to(w_energy[...], (8, CH)).T[:, 0:1]
-
-    def readout(pair, energy):
+
+    for pair in range(5):
+        nodes(pair)
+
+    output_t, output_n = turned[OUTPUT], straight[OUTPUT]
+    weight = jnp.concatenate([w_energy[...], w_energy[...]], axis=1)
+
+    def readout(pair):
         a = 2 * pair
         e = a + 1
         total = jnp.concatenate([hidden[e], hidden[e + 1]], axis=1)
@@ -295,56 +310,81 @@
                 radial_moving(jnp.concatenate([phi[e, here], phi[e + 1, here]], axis=1)),
                 preferred_element_type=F32,
             )
-            edge_radial[a, o] = radial[:, :LAYER]
-            edge_radial[a + 1, o] = radial[:, LAYER:]
             number = LATERAL_OF[(dx, dy)]
             total = total + radial * jnp.concatenate([message[number, e + dz], message[number, e + 1 + dz]], axis=1)
         act, act_slope = silu_parts(product(output_t, total))
         grad = product(output_n, weight * act_slope)
         grad_out[a] = grad[:, :LAYER]
         grad_out[a + 1] = grad[:, LAYER:]
-        part = jnp.sum(weight * act, axis=0, keepdims=True)
-        own = jnp.logical_or(pair == 1, pair == 2)
-        return energy + jnp.where(own, part, 0.0)
-
-    energy = lax.fori_loop(0, 4, readout, jnp.zeros((1, 2 * LAYER), F32))
-
-    message_n = stationary(w_message[...])
-    hidden_n = stationary(w_hidden[...])
-    square_n = stationary(w_square[...])
-    first_n = stationary(w_radial1[...])
-    second_n = stationary(w_radial2[...])
-
-    def back(pair, carry):
+        return jnp.sum(weight * act, axis=0, keepdims=True)
+
+    parts = [readout(pair) for pair in range(4)]
+    energy = parts[1] + parts[2]
+
+    along[0:3] = jnp.where(even, middle[32:35, :], middle[35:38, :])
+    along[3:4] = jnp.where(iota((1, 4 * LAYER), 1) == 0, jnp.sum(energy), 0.0)
+    along[4:8] = jnp.zeros((4, 4 * LAYER), F32)
+
+
+def backward_kernel(
+    reach,
+    inverse_radius,
+    slope,
+    radial_mix,
+    hidden_slope,
+    message,
+    phi,
+    grad_out,
+    straight,
+    radial,
+    radial_turned,
+    forces,
+    grad_summed,
+    pair_grad,
+    pair_grad_turned,
+):
+    row = iota((32, LAYER), 0)
+    site = site_of_row()
+    square_n, hidden_n, message_n = straight[SQUARE], straight[HIDDEN], straight[MESSAGE]
+    first_n, second_n = radial[0], radial[1]
+    second = radial_turned[1]
+
+    def back(pair):
         f = 2 * pair
-        parts = []
-        for k in range(2):
-            grad_message = None
-            for dx, dy in LATERALS:
-                total = None
-                for dz in (-1, 0, 1):
-                    if (dx, dy, dz) == (0, 0, 0):
-                        continue
-                    a = f + k + 1 - dz
-                    term = grad_out[a] * edge_radial[a, ROW_OF[(dx, dy, dz)]]
-                    total = term if total is None else total + term
+        parts = [None, None]
+        for dx, dy in LATERALS:
+            total = None
+            for dz in (-1, 0, 1):
+                if (dx, dy, dz) == (0, 0, 0):
+                    continue
+                a = f + 1 - dz
+                o = ROW_OF[(dx, dy, dz)]
+                here = slice(o * NB, (o + 1) * NB)
+                edge_radial = jnp.dot(
+                    second,
+                    radial_moving(jnp.concatenate([phi[a + 1, here], phi[a + 2, here]], axis=1)),
+                    preferred_element_type=F32,
+                )
+                term = edge_radial * jnp.concatenate([grad_out[a], grad_out[a + 1]], axis=1)
+                total = term if total is None else total + term
+            for k in range(2):
+                part = total[:, k * LAYER : (k + 1) * LAYER]
                 if (dx, dy) != (0, 0):
-                    total = take(total, shifted_site((CH, LAYER), -dx, -dy))
-                grad_message = total if grad_message is None else grad_message + total
-            parts.append(grad_message)
+                    part = take(part, shifted_site((CH, LAYER), -dx, -dy))
+                parts[k] = part if parts[k] is None else parts[k] + part
         grad_hidden = jnp.concatenate([grad_out[f + 1], grad_out[f + 2]], axis=1) + product(
             message_n, jnp.concatenate(parts, axis=1)
         )
-        grad_pre = grad_hidden * jnp.concatenate([hidden_slope[f + 2], hidden_slope[f + 3]], axis=1)
+        grad_pre = grad_hidden * jnp.concatenate([hidden_slope[f], hidden_slope[f + 1]], axis=1)
         grad_mixed = product(hidden_n, grad_pre)
-        mix = jnp.concatenate([radial_mix[f + 2], radial_mix[f + 3]], axis=1)
+        mix = jnp.concatenate([radial_mix[f], radial_mix[f + 1]], axis=1)
         grad_radial = grad_mixed + 2.0 * mix * product(square_n, grad_mixed)
         grad = product(first_n, grad_radial)
         grad_summed[f] = grad[:, :LAYER]
         grad_summed[f + 1] = grad[:, LAYER:]
-        return carry
-
-    lax.fori_loop(0, 3, back, 0)
+
+    for pair in range(3):
+        back(pair)
 
     for f in range(6):
         pair_grad_turned[f] = jnp.zeros((32, LAYER), F32)
@@ -368,7 +408,7 @@
             out.append(jnp.sum(value, axis=0, keepdims=True))
         return out
 
-    def own_edges(pair, carry):
+    def own_edges(pair):
         f = 2 * pair + 1
         for o, offset in enumerate(OFFSETS):
             left, right = edges(f, f + 1, offset, offset)
@@ -376,9 +416,9 @@
             pair_grad[f, o : o + 1] = right
             pair_grad_turned[f, 25 - o : 26 - o] = left
             pair_grad_turned[f + 1, 25 - o : 26 - o] = right
-        return carry
-
-    lax.fori_loop(0, 2, own_edges, 0)
+
+    for pair in range(2):
+        own_edges(pair)
     for dx, dy in LATERALS:
         up, down = (dx, dy, 1), (dx, dy, -1)
         left, right = edges(0, 5, up, down)
@@ -396,40 +436,38 @@
         )
     force = jnp.concatenate(force_parts, axis=1)
 
+    forces[0:3] = force
+    forces[3:8] = jnp.zeros((5, 4 * LAYER), F32)
+
+
+def sums_kernel(parity, middle, forces, along, path, table, kept, sent):
+    even = parity[0] == 0
     low, high = middle[32:35, :], middle[35:38, :]
-    beside = path[0:3, :]
+    force, beside = forces[0:3], path[0:3]
     up = jnp.where(even, high - low, beside - high)
     down = jnp.where(even, low - beside, high - low)
     lane = iota((1, LAYER), 1)
-    values = jnp.zeros((1, LAYER), F32)
-    terms = (
-        energy,
-        force * up,
-        force * down,
-        up * up,
-        down * down,
-        up * down,
-    )
-    for k, term in enumerate(terms):
-        values = values + jnp.where(lane == k, jnp.sum(term), 0.0)
-    sums[...] = values
+    values = jnp.where(
+        lane == 0, along[3:4, 0:1], jnp.where(lane == 6, jnp.broadcast_to(path[3:4, 0:1], (1, LAYER)), 0.0)
+    )
+    for k, term in enumerate((force * up, force * down, up * up, down * down, up * down)):
+        total = jnp.sum(jnp.sum(term, axis=1, keepdims=True), axis=0, keepdims=True)
+        values = values + jnp.where(lane == k + 1, total, 0.0)
+    table[...] = jnp.broadcast_to(values, table.shape)
     both = jnp.concatenate([force, beside, jnp.zeros((2, 4 * LAYER), F32)], axis=0)
     left, right = both[:, : 2 * LAYER], both[:, 2 * LAYER :]
     kept[...] = jnp.where(even, left, right)
     sent[...] = jnp.where(even, right, left)
 
 
-def combine_kernel(image_group, parity, climbing, table, own, kept, received, site_of_slot, out, energies, totals):
+def combine_kernel(images, image_group, parity, climbing, table, own, kept, received, site_of_slot, out, energies):
     even = parity[0] == 0
-    group = image_group[0]
-    groups = table.shape[0] // 32
-    for g in range(groups):
-        total = table[32 * g : 32 * g + 8]
-        for k in range(1, 4):
-            total = total + table[32 * g + 8 * k : 32 * g + 8 * k + 8]
-        total = total[0:4] + total[4:8]
-        totals[2 * g : 2 * g + 2] = total[0:2] + total[2:4]
-    images = 2 * groups
+    total = table[0:8]
+    for k in range(8, table.shape[0], 8):
+        total = total + table[k : k + 8]
+    total = total[0:4] + total[4:8]
+    total = total[0:2] + total[2:4]
+    energy = (total[0:1, 6:7], total[0:1, 0:1], total[1:2, 0:1], total[1:2, 6:7])
     low, high = own[32:35, :], own[35:38, :]
     f_kept, f_received = kept[0:3, :], received[0:3, :]
     p_kept, p_received = kept[3:6, :], received[3:6, :]
@@ -437,13 +475,11 @@
         (jnp.where(even, f_kept, f_received), high - low, low - jnp.where(even, p_kept, p_received)),
         (jnp.where(even, f_received, f_kept), jnp.where(even, p_received, p_kept) - high, high - low),
     )
-    slot = jnp.concatenate([site_of_slot[...]], axis=0)
+    slot = site_of_slot[...]
     for k, (force, up, down) in enumerate(sides):
-        image = 2 * group + k
-        here = totals[pl.ds(image, 1), :]
-        after = totals[pl.ds(jnp.minimum(image + 1, images - 1), 1), :]
-        before = totals[pl.ds(jnp.maximum(image - 1, 0), 1), :]
-        v_here, v_next, v_prev = here[:, 0:1], after[:, 0:1], before[:, 0:1]
+        image = 2 * image_group[0] + k
+        here = total[k : k + 1]
+        v_prev, v_here, v_next = energy[k : k + 3]
         big = jnp.maximum(jnp.abs(v_next - v_here), jnp.abs(v_prev - v_here))
         small = jnp.minimum(jnp.abs(v_next - v_here), jnp.abs(v_prev - v_here))
         rising = jnp.logical_and(v_next > v_here, v_here > v_prev)
@@ -466,7 +502,8 @@
             index = slot[:, part * LAYER : (part + 1) * LAYER]
             low_index = index & (LAYER - 1)
             back = jnp.where(index < LAYER, take(result[:, :LAYER], low_index), take(result[:, LAYER:], low_index))
-            out[k, :, part * LAYER : (part + 1) * LAYER] = back[0:3]
+            for c in range(3):
+                out[c, k : k + 1, part * LAYER : (part + 1) * LAYER] = back[c : c + 1]
         energies[k] = here[0, 0]
 
 
@@ -499,21 +536,84 @@
     even = parity == 0
     parity_arg = parity.astype(I32).reshape(1)
 
+    small = pltpu.CompilerParams(vmem_limit_bytes=4 * 1024 * 1024)
+    packed = jnp.concatenate(
+        [
+            neighbours.reshape(64, LAYER).astype(F32),
+            ghost_slots.astype(F32),
+            positions.transpose(1, 0, 2).reshape(3, 2, 2, LAYER).transpose(0, 2, 1, 3).reshape(12, LAYER),
+        ],
+        axis=0,
+    )
     prepared, site_of_slot = pl.pallas_call(
         prepare_kernel,
         out_shape=(
             jax.ShapeDtypeStruct((ROWS, 2 * LAYER), F32),
             jax.ShapeDtypeStruct((8, 2 * LAYER), I32),
         ),
-        in_specs=[vmem()] * 3,
+        in_specs=[vmem()],
         out_specs=(vmem(), vmem()),
-    )(positions, neighbours.reshape(64, LAYER), ghost_slots)
+        compiler_params=small,
+    )(packed)
 
     mate = lax.ppermute(prepared, "slab", [(i, i ^ 1) for i in range(slabs)])
     middle = jnp.concatenate([jnp.where(even, prepared, mate), jnp.where(even, mate, prepared)], axis=1)
     below = lax.ppermute(middle, "slab", [(i, (i + 2) % slabs) for i in range(slabs)])
     above = lax.ppermute(middle, "slab", [((i + 2) % slabs, i) for i in range(slabs)])
-    mine = jnp.where(even, middle[32:35], middle[35:38])
+
+    def whole(*extents):
+        return jax.ShapeDtypeStruct(extents, F32)
+
+    turned, straight, radial, radial_turned, energy_column = pl.pallas_call(
+        weights_kernel,
+        out_shape=(
+            jax.ShapeDtypeStruct((4, 2 * CH, 2 * CH), BF16),
+            jax.ShapeDtypeStruct((4, 2 * CH, 2 * CH), BF16),
+            jax.ShapeDtypeStruct((2, 2 * NB, 2 * CH), BF16),
+            jax.ShapeDtypeStruct((2, CH, 4 * NB), BF16),
+            whole(CH, CH),
+        ),
+        in_specs=[vmem()] * 2,
+        out_specs=tuple(vmem() for _ in range(5)),
+        compiler_params=small,
+        cost_estimate=pl.CostEstimate(flops=10**8, bytes_accessed=1 << 22, transcendentals=0),
+    )(
+        stacked([w_square, w_hidden, w_message, w_output]),
+        stacked([w_radial1, w_radial2, jnp.broadcast_to(w_energy[None], (NB, CH))]),
+    )
+
+    along, *saved = pl.pallas_call(
+        lambda *refs: forward_kernel(slabs * NZL * LATTICE, *refs),
+        out_shape=(
+            whole(8, 4 * LAYER),
+            whole(4, 3, 32, LAYER),
+            whole(4, 32, LAYER),
+            whole(6, 32 * NB, LAYER),
+            whole(6, CH, LAYER),
+            whole(6, CH, LAYER),
+            whole(9, 10, CH, LAYER),
+            whole(10, 32 * NB, LAYER),
+            whole(8, CH, LAYER),
+        ),
+        in_specs=[smem()] + [vmem()] * 7,
+        out_specs=tuple(vmem() for _ in range(9)),
+        scratch_shapes=[
+            pltpu.VMEM((12, 8, LAYER), F32),
+            pltpu.VMEM((10, NB, LAYER), F32),
+            pltpu.VMEM((10, CH, LAYER), F32),
+        ],
+        compiler_params=pltpu.CompilerParams(vmem_limit_bytes=20 * 1024 * 1024),
+    )(
+        parity_arg,
+        below,
+        middle,
+        above,
+        turned,
+        straight,
+        radial_turned,
+        energy_column,
+    )
+
     hops = []
     for g in range(groups):
         for s in range(slabs):
@@ -521,65 +621,42 @@
                 hops.append((g * slabs + s, (g + 1) * slabs + s - 1))
             if s % 2 == 0 and g > 0:
                 hops.append((g * slabs + s, (g - 1) * slabs + s + 1))
-    path = lax.ppermute(mine, ("image", "slab"), hops)
-
-    kept, sent, sums = pl.pallas_call(
-        lambda *refs: forces_kernel(slabs * NZL * LATTICE, *refs),
-        out_shape=(
-            jax.ShapeDtypeStruct((8, 2 * LAYER), F32),
-            jax.ShapeDtypeStruct((8, 2 * LAYER), F32),
-            jax.ShapeDtypeStruct((1, LAYER), F32),
-        ),
-        in_specs=[smem()] + [vmem()] * 11,
-        out_specs=(vmem(), vmem(), vmem()),
+    path = lax.ppermute(along, ("image", "slab"), hops)
+
+    forces = pl.pallas_call(
+        backward_kernel,
+        out_shape=whole(8, 4 * LAYER),
+        in_specs=[vmem()] * 11,
+        out_specs=vmem(),
         scratch_shapes=[
-            pltpu.VMEM((12, 8, LAYER), F32),
-            pltpu.VMEM((4, 3, 32, LAYER), F32),
-            pltpu.VMEM((4, 32, LAYER), F32),
-            pltpu.VMEM((10, 32 * NB, LAYER), F32),
-            pltpu.VMEM((6, 32 * NB, LAYER), F32),
-            pltpu.VMEM((10, NB, LAYER), F32),
-            pltpu.VMEM((10, CH, LAYER), F32),
-            pltpu.VMEM((10, CH, LAYER), F32),
-            pltpu.VMEM((10, CH, LAYER), F32),
-            pltpu.VMEM((9, 10, CH, LAYER), F32),
-            pltpu.VMEM((8, NOFF, CH, LAYER), F32),
-            pltpu.VMEM((8, CH, LAYER), F32),
             pltpu.VMEM((6, NB, LAYER), F32),
             pltpu.VMEM((4, 32, LAYER), F32),
             pltpu.VMEM((6, 32, LAYER), F32),
         ],
-        compiler_params=pltpu.CompilerParams(vmem_limit_bytes=48 * 1024 * 1024),
-    )(
-        parity_arg,
-        below,
-        middle,
-        above,
-        path,
-        w_radial1,
-        w_square,
-        w_hidden,
-        w_message,
-        w_radial2,
-        w_output,
-        w_energy.reshape(1, CH),
-    )
-
-    devices = groups * slabs
+        compiler_params=pltpu.CompilerParams(vmem_limit_bytes=20 * 1024 * 1024),
+        cost_estimate=pl.CostEstimate(flops=4 * 10**9, bytes_accessed=1 << 22, transcendentals=0),
+    )(*saved, straight, radial, radial_turned)
+
+    table, kept, sent = pl.pallas_call(
+        sums_kernel,
+        out_shape=(whole(slabs, LAYER), whole(8, 2 * LAYER), whole(8, 2 * LAYER)),
+        in_specs=[smem()] + [vmem()] * 4,
+        out_specs=(vmem(), vmem(), vmem()),
+        compiler_params=small,
+    )(parity_arg, middle, forces, along, path)
+
     received = lax.ppermute(sent, "slab", [(i, i ^ 1) for i in range(slabs)])
-    table = lax.all_to_all(
-        jnp.broadcast_to(sums[None], (devices, 1, LAYER)), ("image", "slab"), 0, 0, tiled=False
-    ).reshape(devices, LAYER)
-
-    return pl.pallas_call(
-        combine_kernel,
+    table = lax.all_to_all(table.reshape(slabs, 1, LAYER), "slab", 0, 0, tiled=False).reshape(slabs, LAYER)
+
+    result, energies = pl.pallas_call(
+        lambda *refs: combine_kernel(2 * groups, *refs),
         out_shape=(
-            jax.ShapeDtypeStruct(positions.shape, F32),
+            jax.ShapeDtypeStruct((3, 2, 2 * LAYER), F32),
             jax.ShapeDtypeStruct((2,), F32),
         ),
         in_specs=[smem()] * 3 + [vmem()] * 5,
         out_specs=(vmem(), smem()),
-        scratch_shapes=[pltpu.VMEM((2 * groups, LAYER), F32)],
+        compiler_params=small,
     )(
         group.astype(I32).reshape(1),
         parity_arg,
@@ -590,6 +667,7 @@
         received,
         site_of_slot,
     )
+    return result.transpose(1, 0, 2), energies
 
 
 def solution(mesh):

time: 68.2 us -> 51.6 us (0.76)
  Pallas kernels: 21.8 us -> 15.1 us
  starting transfers between devices: 25.3 us -> 20.7 us
  local copies, waits for them, and re-layouts: 5.16 us -> 0.7 us
  waiting for transfers between devices: 13.3 us -> 9.84 us
  other arithmetic: 0.83 us -> 3.33 us
    pallas_call x2 -> x5, Pallas kernels: 20.1 us -> 14.7 us  [the longest x1 6.79 us: local(): pl.pallas_call(lambda *refs: forward_kernel(slabs * NZL * LATTICE, *refs)...]
    unnamed x21 -> x0, local copies, waits for them, and re-layouts: 3.15 us -> none
    all_to_all x1, starting transfers between devices: 10.5 us -> 7.61 us  [local(): lax.all_to_all(table.reshape(slabs, 1, LAYER), 'slab', 0, 0, tiled=False)]
    ppermute x1, waiting for transfers between devices: 2.23 us -> 0.01 us  [local(): path = lax.ppermute(along, ('image', 'slab'), hops)]
    ppermute x1, starting transfers between devices: 2.23 us -> 0.32 us  [local(): received = lax.ppermute(sent, 'slab', [(i, i ^ 1) for i in range(slabs)])]
    select_n x1 -> x2, other arithmetic: 0.01 us -> 1.84 us  [stacked(): jnp.where(iota(shape, 0) == number, jnp.broadcast_to(array[None], shape),...]
    all_to_all x1, waiting for transfers between devices: 9.8 us -> 8.08 us  [local(): lax.all_to_all(table.reshape(slabs, 1, LAYER), 'slab', 0, 0, tiled=False)]
    ppermute x1, waiting for transfers between devices: 0.01 us -> 1.47 us  [local(): lax.ppermute(middle, 'slab', [(i, (i + 2) % slabs) for i in range(slabs)])]
  transfers between devices with their start and end apart: 6 -> 6, of which waited for: 4 -> 3; matrix products, arithmetic and copies ran while one was open for 0% -> 4% of each run, Pallas kernels for 0% -> 12%
where the time goes in v1:
time: 51.6 us; the launch traced here: 51.2 us
  starting transfers between devices  20.7 us (40%)
  Pallas kernels  15.1 us (29%)
  waiting for transfers between devices  9.84 us (19%)
  other arithmetic  3.33 us (6%)
  between operations  1.55 us (3%)
  local copies, waits for them, and re-layouts  0.7 us (1%)
    all_to_all x1, waiting for transfers between devices, local(): lax.all_to_all(table.reshape(slabs, 1, LAYER), 'slab', 0, 0, tiled=False)  8.08 us
    all_to_all x1, starting transfers between devices, local(): lax.all_to_all(table.reshape(slabs, 1, LAYER), 'slab', 0, 0, tiled=False)  7.61 us
    pallas_call x1, Pallas kernels, local(): pl.pallas_call(lambda *refs: forward_kernel(slabs * NZL * LATTICE, *refs)...  6.79 us
    ppermute x1, starting transfers between devices, local(): lax.ppermute(middle, 'slab', [((i + 2) % slabs, i) for i in range(slabs)])  6.4 us
    pallas_call x1, Pallas kernels, local(): pl.pallas_call(backward_kernel, out_shape=whole(8, 4 * LAYER), in_specs=[...  5.92 us
    ppermute x1, starting transfers between devices, local(): mate = lax.ppermute(prepared, 'slab', [(i, i ^ 1) for i in range(slabs)])  3.33 us
    ppermute x1, starting transfers between devices, local(): path = lax.ppermute(along, ('image', 'slab'), hops)  2.97 us
    select_n x2, other arithmetic, stacked(): jnp.where(iota(shape, 0) == number, jnp.broadcast_to(array[None], shape),...  1.84 us
  transfers between devices with their start and end apart: 6, of which 3 were waited for; matrix products, arithmetic and copies ran while one was open for 4% of the time, Pallas kernels for 12%

profile of v1, /device:TPU:1, one launch (start us, length us, event | category | flops | bytes accessed | tf_op | source)
XLA Modules:
  0.0 51.2 jit_solution(5521035215517846489)
XLA Ops:
  0.6 0.8 %convert_bitcast_fusion = f32[64,128]{1,0:T(8,128)S(1)} fusion(s32[8192]{0:T(1024)} %param.12), kind=kLoop, calls=%fused_computation.3 | loop fusion | flops 8192 | bytes 65536 | tf_op jit(solution)/shard_map/convert_element_type | solution.py:542
  1.4 0.7 %reshape.33 = f32[12,128]{1,0:T(8,128)S(1)} reshape(f32[3,2,2,128]{3,2,1,0:T(2,128)} %bitcast.15) | data formatting | bytes 12288 | tf_op jit(solution)/shard_map/reshape | solution.py:544
  2.1 0.7 %convert_element_type.11 = f32[2,128]{1,0:T(2,128)S(1)} convert(s32[2,128]{1,0:T(2,128)} %param.13) | non-fusion elementwise | flops 256 | bytes 2048 | tf_op jit(solution)/shard_map/convert_element_type | solution.py:543
  2.8 0.4 shard_map.122
  3.2 3.3 %collective-permute-start = (f32[40,256]{1,0:T(8,128)S(1)}, f32[40,256]{1,0:T(8,128)S(1)}, u32[]{:S(2)}, u32[]{:S(2)}) collective-permute-start(f32[40,256]{1,0:T(8,128)S(1)} %get-tuple-element.23.refs_4_), channel_id=1, source_target_pairs={{0,1},{1,0},{2,3},{3,2},{4,5},{5,4},{6,7},{7,6},{8,9},{9,8},{10,11... | collective-permute-start | bytes 122888 | tf_op jit(solution)/shard_map/ppermute | solution.py:559
  6.5 1.1 %select_select_fusion.squares = f32[4,128,128]{2,1,0:T(8,128)S(1)} fusion(f32[128,128]{1,0:T(8,128)} %param.20, f32[128,128]{1,0:T(8,128)} %param.16, f32[128,128]{1,0:T(8,128)} %param.17, f32[128,128]{1,0:T(8,128)} %param.18, pred[4]{0:T(512)(128)(4,1)S(1)} %get-tuple-element.46, pred[4]{0:T(512)(128)(4,1)S(1)} %get-tuple-element.47, ...), kind=kLoop, calls=%fused_computation | loop fusion | flops 196608 | bytes 524300 | tf_op jit(solution)/shard_map/jit(_where)/select_n | solution.py:182
  7.6 0.0 collective-permute-done
  7.6 0.1 collective-permute-start.1
  7.7 6.4 %collective-permute-start.2 = (f32[40,512]{1,0:T(8,128)S(1)}, f32[40,512]{1,0:T(8,128)S(1)}, u32[]{:S(2)}, u32[]{:S(2)}) collective-permute-start(f32[40,512]{1,0:T(8,128)S(1)} %pad_maximum_fusion.refs_2_.middle), channel_id=1, source_target_pairs={{2,0},{3,1},{4,2},{5,3},{6,4},{7,5},{8,6},{9,7},{10,8},{11,9},{12,... | collective-permute-start | bytes 245768 | tf_op jit(solution)/shard_map/ppermute | solution.py:562
  14.1 0.8 %select_select_fusion.1.radials = f32[3,8,128]{2,1,0:T(8,128)S(1)} fusion(f32[128]{0:T(128)} %param.21, f32[8,128]{1,0:T(8,128)} %param.15, f32[8,128]{1,0:T(8,128)} %param.19, pred[3]{0:T(512)(128)(4,1)S(1)} %get-tuple-element.48, pred[3]{0:T(512)(128)(4,1)S(1)} %get-tuple-element.49), kind=kLoop, calls=%fused_computation.6 | loop fusion | flops 6144 | bytes 20998 | tf_op jit(solution)/shard_map/jit(_where)/select_n | solution.py:182
  14.9 0.3 shard_map.123
  15.3 1.5 %collective-permute-done.1.refs_1_ = f32[40,512]{1,0:T(8,128)S(1)} collective-permute-done((f32[40,512]{1,0:T(8,128)S(1)}, f32[40,512]{1,0:T(8,128)S(1)}, u32[]{:S(2)}, u32[]{:S(2)}) %collective-permute-start.1) | collective-permute-done | bytes 81952 | tf_op jit(solution)/shard_map/ppermute | solution.py:561
  16.7 0.0 collective-permute-done.2.refs_3_
  16.7 6.8 %shard_map.124 = (f32[8,512]{1,0:T(8,128)S(1)}, f32[4,3,32,128]{3,2,1,0:T(8,128)S(1)}, f32[4,32,128]{2,1,0:T(8,128)S(1)}, f32[6,256,128]{2,1,0:T(8,128)S(1)}, f3...) custom-call(s32[1]{0:T(128)} %bitcast.1.refs_0_.parity.refs_1_, ...), custom_call_target="tpu_custom_call" | custom-call | tf_op jit(solution)/shard_map/pallas_call | solution.py:585
  23.5 3.0 %collective-permute-start.3 = (f32[8,512]{1,0:T(8,128)S(1)}, f32[8,512]{1,0:T(8,128)S(1)}, u32[]{:S(2)}, u32[]{:S(2)}) collective-permute-start(f32[8,512]{1,0:T(8,128)S(1)} %get-tuple-element.37.along), channel_id=1, source_target_pairs={{1,32},{3,34},{5,36},{7,38},{9,40},{11,42},{13,44},{15,46},{17,48}... | collective-permute-start | bytes 49160 | tf_op jit(solution)/shard_map/ppermute | solution.py:624
  26.5 5.9 %shard_map.125.forces = f32[8,512]{1,0:T(8,128)S(1)} custom-call(f32[4,3,32,128]{3,2,1,0:T(8,128)S(1)} %get-tuple-element.28.reach, f32[4,32,128]{2,1,0:T(8,128)S(1)} %get-tuple-element.29.inverse_radius, f32[6,256,128]{2,1,0:T(8,128)S(1)} %get-tuple-element.30.slope, f32[6,128,128]{2,1,0:T(8,128)S(1)} %get-tuple-element.31.radial_mix, ...), custom_call_target="tpu_custom_call" | custom-call | flops 4000000000 | bytes 4194304 | tf_op jit(solution)/shard_map/pallas_call | solution.py:626
  32.4 0.0 collective-permute-done.3.path
  32.4 0.7 %shard_map.126 = (f32[32,128]{1,0:T(8,128)}, f32[8,256]{1,0:T(8,128)S(1)}, f32[8,256]{1,0:T(8,128)S(1)}) custom-call(s32[1]{0:T(128)} %bitcast.1.refs_0_.parity.refs_1_, f32[40,512]{1,0:T(8,128)S(1)} %pad_maximum_fusion.refs_2_.middle, f32[8,512]{1,0:T(8,128)S(1)} %shard_map.125.forces, f32[8,512]{1,0:T(8,128)S(1)} %get-tuple-element.37.along, ...), custom_call_target="tpu_custom_call" | custom-call | tf_op jit(solution)/shard_map/pallas_call | solution.py:640
  33.2 7.6 %all-to-all-start = ((f32[32,1,128]{2,1,0:T(1,128)}), f32[32,1,128]{2,1,0:T(1,128)S(1)}, u32[]{:S(2)}, u32[]{:S(2)}) async-start(f32[32,1,128]{2,1,0:T(1,128)} %bitcast.7), calls=%async_computation | async-start | bytes 32768 | tf_op jit(solution)/shard_map/all_to_all | solution.py:649
  40.8 0.3 collective-permute-start.4
  41.8 0.3 collective-permute-done.4.refs_6_
  42.1 8.1 %all-to-all-done = f32[32,1,128]{2,1,0:T(1,128)S(1)} async-done(((f32[32,1,128]{2,1,0:T(1,128)}), f32[32,1,128]{2,1,0:T(1,128)S(1)}, u32[]{:S(2)}, u32[]{:S(2)}) %all-to-all-start) | async-done | bytes 16416 | tf_op jit(solution)/shard_map/all_to_all | solution.py:649
  50.1 0.9 %shard_map.127 = (f32[3,2,256]{2,1,0:T(2,128)}, f32[2]{0:T(128)}) custom-call(s32[1]{0:T(128)} %bitcast.refs_0_, s32[1]{0:T(128)} %bitcast.1.refs_0_.parity.refs_1_, s32[1]{0:T(128)S(6)} %copy.16.refs_2_, f32[32,128]{1,0:T(8,128)S(1)} %bitcast.14, f32[40,256]{1,0:T(8,128)S(1)} %get-tuple-element.23.refs_4_, f32[8,256]{1,0:T(8,128)S(1)} %get-tuple-element.39.refs_5_, ...), custom_call_target="tpu_custom_call" | custom-call | tf_op jit(solution)/shard_map/pallas_call | solution.py:651
  (6 shorter events, 0.0 us)
Async XLA Ops:
  3.2 4.4 %collective-permute-start = (f32[40,256]{1,0:T(8,128)S(1)}, f32[40,256]{1,0:T(8,128)S(1)}, u32[]{:S(2)}, u32[]{:S(2)}) collective-permute-start(f32[40,256]{1,0:T(8,128)S(1)} %get-tuple-element.23.refs_4_), channel_id=1, source_target_pairs={{0,1},{1,0},{2,3},{3,2},{4,5},{5,4},{6,7},{7,6},{8,9},{9,8},{10,11... | collective-permute-start | bytes 122888 | tf_op jit(solution)/shard_map/ppermute | solution.py:559
  7.6 9.1 %collective-permute-start.1 = (f32[40,512]{1,0:T(8,128)S(1)}, f32[40,512]{1,0:T(8,128)S(1)}, u32[]{:S(2)}, u32[]{:S(2)}) collective-permute-start(f32[40,512]{1,0:T(8,128)S(1)} %pad_maximum_fusion.refs_2_.middle), channel_id=1, source_target_pairs={{0,2},{1,3},{2,4},{3,5},{4,6},{5,7},{6,8},{7,9},{8,10},{9,11},{10,... | collective-permute-start | bytes 245768 | tf_op jit(solution)/shard_map/ppermute | solution.py:561
  7.7 9.0 %collective-permute-start.2 = (f32[40,512]{1,0:T(8,128)S(1)}, f32[40,512]{1,0:T(8,128)S(1)}, u32[]{:S(2)}, u32[]{:S(2)}) collective-permute-start(f32[40,512]{1,0:T(8,128)S(1)} %pad_maximum_fusion.refs_2_.middle), channel_id=1, source_target_pairs={{2,0},{3,1},{4,2},{5,3},{6,4},{7,5},{8,6},{9,7},{10,8},{11,9},{12,... | collective-permute-start | bytes 245768 | tf_op jit(solution)/shard_map/ppermute | solution.py:562
  23.5 8.9 %collective-permute-start.3 = (f32[8,512]{1,0:T(8,128)S(1)}, f32[8,512]{1,0:T(8,128)S(1)}, u32[]{:S(2)}, u32[]{:S(2)}) collective-permute-start(f32[8,512]{1,0:T(8,128)S(1)} %get-tuple-element.37.along), channel_id=1, source_target_pairs={{1,32},{3,34},{5,36},{7,38},{9,40},{11,42},{13,44},{15,46},{17,48}... | collective-permute-start | bytes 49160 | tf_op jit(solution)/shard_map/ppermute | solution.py:624
  33.2 17.0 %all-to-all-start = ((f32[32,1,128]{2,1,0:T(1,128)}), f32[32,1,128]{2,1,0:T(1,128)S(1)}, u32[]{:S(2)}, u32[]{:S(2)}) async-start(f32[32,1,128]{2,1,0:T(1,128)} %bitcast.7), calls=%async_computation | async-start | bytes 32768 | tf_op jit(solution)/shard_map/all_to_all | solution.py:649
  40.8 1.3 %collective-permute-start.4 = (f32[8,256]{1,0:T(8,128)S(1)}, f32[8,256]{1,0:T(8,128)S(1)}, u32[]{:S(2)}, u32[]{:S(2)}) collective-permute-start(f32[8,256]{1,0:T(8,128)S(1)} %get-tuple-element.40), channel_id=1, source_target_pairs={{0,1},{1,0},{2,3},{3,2},{4,5},{5,4},{6,7},{7,6},{8,9},{9,8},{10,11... | collective-permute-start | bytes 24584 | tf_op jit(solution)/shard_map/ppermute | solution.py:648

commit v2 on v1

--- a/solution.py
+++ b/solution.py
@@ -14,7 +14,7 @@
 LAYER = 128
 CH = 128
 NOFF = 26
-ROWS = 40
+ROWS = 32
 
 LATTICE = 2.55
 CUTOFF = 5.0
@@ -94,8 +94,8 @@
     return jnp.concatenate([both, both], axis=0)
 
 
-def prepare_kernel(packed, out, site_of_slot):
-    slots = packed[64:66, :].astype(I32)
+def prepare_kernel(packed, positions, out, site_of_slot):
+    slots = packed[64:66, :]
     inverse = jnp.zeros((8, 2 * LAYER), F32)
     for layer in range(NZL):
         hit = (jnp.broadcast_to(slots[layer : layer + 1], (2 * LAYER, LAYER)) == iota((2 * LAYER, LAYER), 0))
@@ -112,13 +112,13 @@
     second = jnp.broadcast_to(inverse[0:1, LAYER:], (32, LAYER))
     sides = [
         jnp.concatenate(
-            [packed[66 + 4 * c + 2 * half + k : 67 + 4 * c + 2 * half + k] for k in range(2) for c in range(3)]
+            [positions[c, k : k + 1, half * LAYER : (half + 1) * LAYER] for k in range(2) for c in range(3)]
             + [jnp.zeros((2, LAYER), F32)],
             axis=0,
         )
         for half in range(2)
     ]
-    listed = packed[0:64, :]
+    listed = packed[0:64, :].astype(F32)
     turned = jnp.concatenate([listed, jnp.zeros((64, LAYER), F32)], axis=0).T
     site = iota((32, LAYER), 1)
     row = iota((32, LAYER), 0)
@@ -126,7 +126,7 @@
         here = slice(layer * LAYER, (layer + 1) * LAYER)
         slot = jnp.broadcast_to(slots[layer : layer + 1], (8, LAYER))
         low = slot & (LAYER - 1)
-        out[32:40, here] = jnp.where(slot < LAYER, take(sides[0], low), take(sides[1], low))
+        coords = jnp.where(slot < LAYER, take(sides[0], low), take(sides[1], low))
         slot = jnp.broadcast_to(slots[layer : layer + 1], (32, LAYER))
         picked = take(turned[0:32], slot >> 2)
         for part in range(1, 4):
@@ -148,7 +148,8 @@
         bits = bits[0:2] | bits[2:4]
         bits = bits[0:1] | bits[1:2]
         mask = (jnp.broadcast_to(bits, (32, LAYER)) >> row) & 1
-        out[0:32, here] = jnp.where(row < NOFF, mask.astype(F32), 0.0)
+        out[0:NOFF, here] = mask[0:NOFF].astype(F32)
+        out[NOFF:32, here] = coords[0:6]
 
 
 SIN_TERMS = [(-1.0) ** k / math.factorial(2 * k + 1) for k in range(7)]
@@ -186,9 +187,9 @@
 def forward_kernel(
     cell_z,
     parity,
-    below,
+    far,
     middle,
-    above,
+    traded,
     turned,
     straight,
     radial_turned,
@@ -207,16 +208,23 @@
     hidden,
 ):
     even = parity[0] == 0
-    blocks = [(ref, slice(k * LAYER, (k + 1) * LAYER)) for ref in (below, middle, above) for k in range(4)]
-    for level, (ref, here) in enumerate(blocks):
-        coords[level, 0:3] = jnp.where(even, ref[32:35, here], ref[35:38, here])
+
+    def level_rows(level, first, last):
+        here = slice(level % 4 * LAYER, (level % 4 + 1) * LAYER)
+        if 4 <= level < 8:
+            return middle[first:last, here]
+        mine, other = far[first:last, here], traded[first:last, here]
+        return jnp.where(even, mine, other) if level < 4 else jnp.where(even, other, mine)
+
+    for level in range(12):
+        both = level_rows(level, 24, 32)
+        coords[level, 0:3] = jnp.where(even, both[2:5], both[5:8])
     row = iota((32, LAYER), 0)
     site = site_of_row()
     boxes = (NX * LATTICE, NY * LATTICE, cell_z)
 
     for e in range(10):
-        ref, here = blocks[e + 1]
-        mask = ref[0:32, here]
+        mask = jnp.where(row < NOFF, level_rows(e + 1, 0, 32), 0.0)
         squared = None
         for c in range(3):
             centre = coords[e + 1, c : c + 1]
@@ -271,33 +279,27 @@
     first, second = radial_turned[0], radial_turned[1]
     square_t, hidden_t, message_t = turned[SQUARE], turned[HIDDEN], turned[MESSAGE]
 
-    def nodes(pair):
-        e = 2 * pair
-        mix = jnp.dot(
-            first,
-            radial_moving(jnp.concatenate([summed[e], summed[e + 1]], axis=1)),
-            preferred_element_type=F32,
-        )
-        mixed = mix + product(square_t, mix * mix)
-        act, act_slope = silu_parts(product(hidden_t, mixed))
-        sent_on = product(message_t, act)
-        for k in range(2):
-            here = slice(k * LAYER, (k + 1) * LAYER)
-            hidden[e + k] = act[:, here]
-            if 2 <= e <= 6:
-                radial_mix[e + k - 2] = mix[:, here]
-                hidden_slope[e + k - 2] = act_slope[:, here]
-            for number, (dx, dy) in enumerate(LATERALS):
-                part = sent_on[:, here]
-                if (dx, dy) != (0, 0):
-                    part = take(part, shifted_site((CH, LAYER), dx, dy))
-                message[number, e + k] = part
-
-    for pair in range(5):
-        nodes(pair)
+    mix = jnp.dot(
+        first,
+        radial_moving(jnp.concatenate([summed[e] for e in range(10)], axis=1)),
+        preferred_element_type=F32,
+    )
+    mixed = mix + product(square_t, mix * mix)
+    act, act_slope = silu_parts(product(hidden_t, mixed))
+    sent_on = product(message_t, act)
+    for e in range(10):
+        here = slice(e * LAYER, (e + 1) * LAYER)
+        hidden[e] = act[:, here]
+        if 2 <= e <= 7:
+            radial_mix[e - 2] = mix[:, here]
+            hidden_slope[e - 2] = act_slope[:, here]
+        for number, (dx, dy) in enumerate(LATERALS):
+            part = sent_on[:, here]
+            if (dx, dy) != (0, 0):
+                part = take(part, shifted_site((CH, LAYER), dx, dy))
+            message[number, e] = part
 
     output_t, output_n = turned[OUTPUT], straight[OUTPUT]
-    weight = jnp.concatenate([w_energy[...], w_energy[...]], axis=1)
 
     def readout(pair):
         a = 2 * pair
@@ -312,16 +314,18 @@
             )
             number = LATERAL_OF[(dx, dy)]
             total = total + radial * jnp.concatenate([message[number, e + dz], message[number, e + 1 + dz]], axis=1)
-        act, act_slope = silu_parts(product(output_t, total))
-        grad = product(output_n, weight * act_slope)
-        grad_out[a] = grad[:, :LAYER]
-        grad_out[a + 1] = grad[:, LAYER:]
-        return jnp.sum(weight * act, axis=0, keepdims=True)
-
-    parts = [readout(pair) for pair in range(4)]
-    energy = parts[1] + parts[2]
-
-    along[0:3] = jnp.where(even, middle[32:35, :], middle[35:38, :])
+        return total
+
+    total = jnp.concatenate([readout(pair) for pair in range(4)], axis=1)
+    weight = jnp.concatenate([w_energy[...]] * 8, axis=1)
+    act, act_slope = silu_parts(product(output_t, total))
+    grad = product(output_n, weight * act_slope)
+    for a in range(8):
+        grad_out[a] = grad[:, a * LAYER : (a + 1) * LAYER]
+    own = slice(2 * LAYER, 6 * LAYER)
+    energy = jnp.sum(weight[:, own] * act[:, own], axis=0, keepdims=True)
+
+    along[0:3] = jnp.where(even, middle[26:29, :], middle[29:32, :])
     along[3:4] = jnp.where(iota((1, 4 * LAYER), 1) == 0, jnp.sum(energy), 0.0)
     along[4:8] = jnp.zeros((4, 4 * LAYER), F32)
 
@@ -372,19 +376,16 @@
                 if (dx, dy) != (0, 0):
                     part = take(part, shifted_site((CH, LAYER), -dx, -dy))
                 parts[k] = part if parts[k] is None else parts[k] + part
-        grad_hidden = jnp.concatenate([grad_out[f + 1], grad_out[f + 2]], axis=1) + product(
-            message_n, jnp.concatenate(parts, axis=1)
-        )
-        grad_pre = grad_hidden * jnp.concatenate([hidden_slope[f], hidden_slope[f + 1]], axis=1)
-        grad_mixed = product(hidden_n, grad_pre)
-        mix = jnp.concatenate([radial_mix[f], radial_mix[f + 1]], axis=1)
-        grad_radial = grad_mixed + 2.0 * mix * product(square_n, grad_mixed)
-        grad = product(first_n, grad_radial)
-        grad_summed[f] = grad[:, :LAYER]
-        grad_summed[f + 1] = grad[:, LAYER:]
-
-    for pair in range(3):
-        back(pair)
+        return jnp.concatenate(parts, axis=1)
+
+    grad_message = jnp.concatenate([back(pair) for pair in range(3)], axis=1)
+    grad_hidden = jnp.concatenate([grad_out[a] for a in range(1, 7)], axis=1) + product(message_n, grad_message)
+    grad_pre = grad_hidden * jnp.concatenate([hidden_slope[f] for f in range(6)], axis=1)
+    grad_mixed = product(hidden_n, grad_pre)
+    mix = jnp.concatenate([radial_mix[f] for f in range(6)], axis=1)
+    grad = product(first_n, grad_mixed + 2.0 * mix * product(square_n, grad_mixed))
+    for f in range(6):
+        grad_summed[f] = grad[:, f * LAYER : (f + 1) * LAYER]
 
     for f in range(6):
         pair_grad_turned[f] = jnp.zeros((32, LAYER), F32)
@@ -442,7 +443,7 @@
 
 def sums_kernel(parity, middle, forces, along, path, table, kept, sent):
     even = parity[0] == 0
-    low, high = middle[32:35, :], middle[35:38, :]
+    low, high = middle[26:29, :], middle[29:32, :]
     force, beside = forces[0:3], path[0:3]
     up = jnp.where(even, high - low, beside - high)
     down = jnp.where(even, low - beside, high - low)
@@ -468,7 +469,7 @@
     total = total[0:4] + total[4:8]
     total = total[0:2] + total[2:4]
     energy = (total[0:1, 6:7], total[0:1, 0:1], total[1:2, 0:1], total[1:2, 6:7])
-    low, high = own[32:35, :], own[35:38, :]
+    low, high = own[26:29, :], own[29:32, :]
     f_kept, f_received = kept[0:3, :], received[0:3, :]
     p_kept, p_received = kept[3:6, :], received[3:6, :]
     sides = (
@@ -537,30 +538,23 @@
     parity_arg = parity.astype(I32).reshape(1)
 
     small = pltpu.CompilerParams(vmem_limit_bytes=4 * 1024 * 1024)
-    packed = jnp.concatenate(
-        [
-            neighbours.reshape(64, LAYER).astype(F32),
-            ghost_slots.astype(F32),
-            positions.transpose(1, 0, 2).reshape(3, 2, 2, LAYER).transpose(0, 2, 1, 3).reshape(12, LAYER),
-        ],
-        axis=0,
-    )
+    packed = jnp.concatenate([neighbours.reshape(64, LAYER), ghost_slots], axis=0)
     prepared, site_of_slot = pl.pallas_call(
         prepare_kernel,
         out_shape=(
             jax.ShapeDtypeStruct((ROWS, 2 * LAYER), F32),
             jax.ShapeDtypeStruct((8, 2 * LAYER), I32),
         ),
-        in_specs=[vmem()],
+        in_specs=[vmem()] * 2,
         out_specs=(vmem(), vmem()),
         compiler_params=small,
-    )(packed)
+    )(packed, positions.transpose(1, 0, 2))
 
     mate = lax.ppermute(prepared, "slab", [(i, i ^ 1) for i in range(slabs)])
     middle = jnp.concatenate([jnp.where(even, prepared, mate), jnp.where(even, mate, prepared)], axis=1)
-    below = lax.ppermute(middle, "slab", [(i, (i + 2) % slabs) for i in range(slabs)])
-    above = lax.ppermute(middle, "slab", [((i + 2) % slabs, i) for i in range(slabs)])
-
+    far = lax.ppermute(
+        middle, "slab", [(i, (i + 2) % slabs) if i % 2 == 0 else (i, (i - 2) % slabs) for i in range(slabs)]
+    )
     def whole(*extents):
         return jax.ShapeDtypeStruct(extents, F32)
 
@@ -581,6 +575,9 @@
         stacked([w_square, w_hidden, w_message, w_output]),
         stacked([w_radial1, w_radial2, jnp.broadcast_to(w_energy[None], (NB, CH))]),
     )
+
+    far, turned, straight = lax.optimization_barrier((far, turned, straight))
+    traded = lax.ppermute(far, "slab", [(i, i ^ 1) for i in range(slabs)])
 
     along, *saved = pl.pallas_call(
         lambda *refs: forward_kernel(slabs * NZL * LATTICE, *refs),
@@ -605,9 +602,9 @@
         compiler_params=pltpu.CompilerParams(vmem_limit_bytes=20 * 1024 * 1024),
     )(
         parity_arg,
-        below,
+        far,
         middle,
-        above,
+        traded,
         turned,
         straight,
         radial_turned,

time: 51.6 us -> 47.2 us (0.915)
  Pallas kernels: 15.1 us -> 12.2 us
  other arithmetic: 3.33 us -> 2.65 us
    pallas_call x1, Pallas kernels: 5.92 us -> 4.18 us  [local(): pl.pallas_call(backward_kernel, out_shape=whole(8, 4 * LAYER), in_specs=[...]
    convert_element_type x2 -> x0, other arithmetic: 1.44 us -> none  [the longest x1 0.76 us: local(): neighbours.reshape(64, LAYER).astype(F32)]
    pallas_call x1, Pallas kernels: 6.79 us -> 5.57 us  [local(): pl.pallas_call(lambda *refs: forward_kernel(slabs * NZL * LATTICE, *refs)...]
    ppermute x2, starting transfers between devices: 6.49 us -> 7.67 us  [the longest x1 6.38 us: local(): lax.ppermute(middle, 'slab', [(i, (i + 2) % slabs) if i % 2 == 0 else (i,...]
    all_to_all x1, starting transfers between devices: 7.61 us -> 6.72 us  [local(): lax.all_to_all(table.reshape(slabs, 1, LAYER), 'slab', 0, 0, tiled=False)]
    concatenate x1, other arithmetic: 0.01 us -> 0.78 us  [local(): jnp.concatenate([neighbours.reshape(64, LAYER), ghost_slots], axis=0)]
    reshape x1 -> x0, local copies, waits for them, and re-layouts: 0.7 us -> none  [local(): positions.transpose(1, 0, 2).reshape(3, 2, 2, LAYER).transpose(0, 2, 1, 3)]
    unnamed x0 -> x2, local copies, waits for them, and re-layouts: none -> 0.69 us
  transfers between devices with their start and end apart: 6 -> 6, of which waited for: 3 -> 4; matrix products, arithmetic and copies ran while one was open for 4% -> 4% of each run, Pallas kernels for 12% -> 10%
where the time goes in v2:
time: 47.2 us; the launch traced here: 46.8 us
  starting transfers between devices  20.5 us (43%)
  Pallas kernels  12.2 us (26%)
  waiting for transfers between devices  9.48 us (20%)
  other arithmetic  2.65 us (6%)
  between operations  1.38 us (3%)
  local copies, waits for them, and re-layouts  0.69 us (1%)
    all_to_all x1, waiting for transfers between devices, local(): lax.all_to_all(table.reshape(slabs, 1, LAYER), 'slab', 0, 0, tiled=False)  8.08 us
    all_to_all x1, starting transfers between devices, local(): lax.all_to_all(table.reshape(slabs, 1, LAYER), 'slab', 0, 0, tiled=False)  6.72 us
    ppermute x1, starting transfers between devices, local(): lax.ppermute(middle, 'slab', [(i, (i + 2) % slabs) if i % 2 == 0 else (i,...  6.38 us
    pallas_call x1, Pallas kernels, local(): pl.pallas_call(lambda *refs: forward_kernel(slabs * NZL * LATTICE, *refs)...  5.57 us
    pallas_call x1, Pallas kernels, local(): pl.pallas_call(backward_kernel, out_shape=whole(8, 4 * LAYER), in_specs=[...  4.18 us
    ppermute x1, starting transfers between devices, local(): mate = lax.ppermute(prepared, 'slab', [(i, i ^ 1) for i in range(slabs)])  3.33 us
    ppermute x1, starting transfers between devices, local(): path = lax.ppermute(along, ('image', 'slab'), hops)  2.46 us
    select_n x2, other arithmetic, stacked(): jnp.where(iota(shape, 0) == number, jnp.broadcast_to(array[None], shape),...  1.84 us
  transfers between devices with their start and end apart: 6, of which 4 were waited for; matrix products, arithmetic and copies ran while one was open for 4% of the time, Pallas kernels for 10%

profile of v2, /device:TPU:1, one launch (start us, length us, event | category | flops | bytes accessed | tf_op | source)
XLA Modules:
  0.0 46.8 jit_solution(15958993170442884593)
XLA Ops:
  0.6 0.8 %pad_add_fusion.packed = s32[66,128]{1,0:T(8,128)S(1)} fusion(s32[2,128]{1,0:T(2,128)} %param.13, s32[64,128]{1,0:T(8,128)} %bitcast.11), kind=kLoop, calls=%fused_computation.2 | loop fusion | flops 8448 | bytes 67584 | tf_op jit(solution)/shard_map/concatenate | solution.py:541
  1.4 0.0 copy-start
  1.4 0.7 %copy-done = f32[2,3,256]{2,0,1:T(2,128)S(1)} copy-done((f32[2,3,256]{2,0,1:T(2,128)S(1)}, f32[2,3,256]{2,0,1:T(2,128)}, u32[]{:S(2)}) %copy-start) | copy-done | bytes 6168
  2.1 0.4 shard_map.122
  2.5 3.3 %collective-permute-start = (f32[32,256]{1,0:T(8,128)S(1)}, f32[32,256]{1,0:T(8,128)S(1)}, u32[]{:S(2)}, u32[]{:S(2)}) collective-permute-start(f32[32,256]{1,0:T(8,128)S(1)} %get-tuple-element.26.refs_4_), channel_id=1, source_target_pairs={{0,1},{1,0},{2,3},{3,2},{4,5},{5,4},{6,7},{7,6},{8,9},{9,8},{10,11... | collective-permute-start | bytes 98312 | tf_op jit(solution)/shard_map/ppermute | solution.py:553
  5.8 1.1 %select_select_fusion.squares = f32[4,128,128]{2,1,0:T(8,128)S(1)} fusion(f32[128,128]{1,0:T(8,128)} %param.20, f32[128,128]{1,0:T(8,128)} %param.16, f32[128,128]{1,0:T(8,128)} %param.17, f32[128,128]{1,0:T(8,128)} %param.18, pred[4]{0:T(512)(128)(4,1)S(1)} %get-tuple-element.52, pred[4]{0:T(512)(128)(4,1)S(1)} %get-tuple-element.53, ...), kind=kLoop, calls=%fused_computation | loop fusion | flops 196608 | bytes 524300 | tf_op jit(solution)/shard_map/jit(_where)/select_n | solution.py:183
  6.9 0.0 collective-permute-done
  7.0 6.4 %collective-permute-start.1 = (f32[32,512]{1,0:T(8,128)S(1)}, f32[32,512]{1,0:T(8,128)S(1)}, u32[]{:S(2)}, u32[]{:S(2)}) collective-permute-start(f32[32,512]{1,0:T(8,128)S(1)} %pad_maximum_fusion.refs_2_.middle), channel_id=1, source_target_pairs={{0,2},{1,31},{2,4},{3,1},{4,6},{5,3},{6,8},{7,5},{8,10},{9,7},{10,... | collective-permute-start | bytes 196616 | tf_op jit(solution)/shard_map/ppermute | solution.py:555
  13.3 0.8 %select_select_fusion.1.radials = f32[3,8,128]{2,1,0:T(8,128)S(1)} fusion(f32[128]{0:T(128)} %param.21, f32[8,128]{1,0:T(8,128)} %param.15, f32[8,128]{1,0:T(8,128)} %param.19, pred[3]{0:T(512)(128)(4,1)S(1)} %get-tuple-element.54, pred[3]{0:T(512)(128)(4,1)S(1)} %get-tuple-element.55), kind=kLoop, calls=%fused_computation.5 | loop fusion | flops 6144 | bytes 20998 | tf_op jit(solution)/shard_map/jit(_where)/select_n | solution.py:183
  14.1 0.3 shard_map.123
  14.5 0.2 collective-permute-done.1.refs_1_
  14.7 1.3 %collective-permute-start.2 = (f32[32,512]{1,0:T(8,128)S(1)}, f32[32,512]{1,0:T(8,128)S(1)}, u32[]{:S(2)}, u32[]{:S(2)}) collective-permute-start(f32[32,512]{1,0:T(8,128)S(1)} %collective-permute-done.1.refs_1_), channel_id=1, source_target_pairs={{0,1},{1,0},{2,3},{3,2},{4,5},{5,4},{6,7},{7,6},{8,9},{9,8},{10,11... | collective-permute-start | bytes 196616 | tf_op jit(solution)/shard_map/ppermute | solution.py:580
  16.0 0.9 %collective-permute-done.2.refs_3_ = f32[32,512]{1,0:T(8,128)S(1)} collective-permute-done((f32[32,512]{1,0:T(8,128)S(1)}, f32[32,512]{1,0:T(8,128)S(1)}, u32[]{:S(2)}, u32[]{:S(2)}) %collective-permute-start.2) | collective-permute-done | bytes 65568 | tf_op jit(solution)/shard_map/ppermute | solution.py:580
  16.9 5.6 %shard_map.124 = (f32[8,512]{1,0:T(8,128)S(1)}, f32[4,3,32,128]{3,2,1,0:T(8,128)S(1)}, f32[4,32,128]{2,1,0:T(8,128)S(1)}, f32[6,256,128]{2,1,0:T(8,128)S(1)}, f3...) custom-call(s32[1]{0:T(128)} %bitcast.1.refs_0_.parity.refs_1_, ...), custom_call_target="tpu_custom_call" | custom-call | tf_op jit(solution)/shard_map/pallas_call | solution.py:582
  22.4 2.5 %collective-permute-start.3 = (f32[8,512]{1,0:T(8,128)S(1)}, f32[8,512]{1,0:T(8,128)S(1)}, u32[]{:S(2)}, u32[]{:S(2)}) collective-permute-start(f32[8,512]{1,0:T(8,128)S(1)} %get-tuple-element.43.along), channel_id=1, source_target_pairs={{1,32},{3,34},{5,36},{7,38},{9,40},{11,42},{13,44},{15,46},{17,48}... | collective-permute-start | bytes 49160 | tf_op jit(solution)/shard_map/ppermute | solution.py:621
  24.9 4.2 %shard_map.125.forces = f32[8,512]{1,0:T(8,128)S(1)} custom-call(f32[4,3,32,128]{3,2,1,0:T(8,128)S(1)} %get-tuple-element.34.reach, f32[4,32,128]{2,1,0:T(8,128)S(1)} %get-tuple-element.35.inverse_radius, f32[6,256,128]{2,1,0:T(8,128)S(1)} %get-tuple-element.36.slope, f32[6,128,128]{2,1,0:T(8,128)S(1)} %get-tuple-element.37.radial_mix, ...), custom_call_target="tpu_custom_call" | custom-call | flops 4000000000 | bytes 4194304 | tf_op jit(solution)/shard_map/pallas_call | solution.py:623
  29.1 0.0 collective-permute-done.3.path
  29.1 0.7 %shard_map.126 = (f32[32,128]{1,0:T(8,128)}, f32[8,256]{1,0:T(8,128)S(1)}, f32[8,256]{1,0:T(8,128)S(1)}) custom-call(s32[1]{0:T(128)} %bitcast.1.refs_0_.parity.refs_1_, f32[32,512]{1,0:T(8,128)S(1)} %pad_maximum_fusion.refs_2_.middle, f32[8,512]{1,0:T(8,128)S(1)} %shard_map.125.forces, f32[8,512]{1,0:T(8,128)S(1)} %get-tuple-element.43.along, ...), custom_call_target="tpu_custom_call" | custom-call | tf_op jit(solution)/shard_map/pallas_call | solution.py:637
  29.8 6.7 %all-to-all-start = ((f32[32,1,128]{2,1,0:T(1,128)}), f32[32,1,128]{2,1,0:T(1,128)S(1)}, u32[]{:S(2)}, u32[]{:S(2)}) async-start(f32[32,1,128]{2,1,0:T(1,128)} %bitcast.5), calls=%async_computation | async-start | bytes 32768 | tf_op jit(solution)/shard_map/all_to_all | solution.py:646
  36.6 0.3 collective-permute-start.4
  37.5 0.3 collective-permute-done.4.refs_6_
  37.8 8.1 %all-to-all-done = f32[32,1,128]{2,1,0:T(1,128)S(1)} async-done(((f32[32,1,128]{2,1,0:T(1,128)}), f32[32,1,128]{2,1,0:T(1,128)S(1)}, u32[]{:S(2)}, u32[]{:S(2)}) %all-to-all-start) | async-done | bytes 16416 | tf_op jit(solution)/shard_map/all_to_all | solution.py:646
  45.9 0.9 %shard_map.127 = (f32[3,2,256]{2,1,0:T(2,128)}, f32[2]{0:T(128)}) custom-call(s32[1]{0:T(128)} %bitcast.refs_0_, s32[1]{0:T(128)} %bitcast.1.refs_0_.parity.refs_1_, s32[1]{0:T(128)S(6)} %copy.14.refs_2_, f32[32,128]{1,0:T(8,128)S(1)} %bitcast.9, f32[32,256]{1,0:T(8,128)S(1)} %get-tuple-element.26.refs_4_, f32[8,256]{1,0:T(8,128)S(1)} %get-tuple-element.45.refs_5_, ...), custom_call_target="tpu_custom_call" | custom-call | tf_op jit(solution)/shard_map/pallas_call | solution.py:648
  (5 shorter events, 0.0 us)
Async XLA Ops:
  1.4 0.7 %copy-start = (f32[2,3,256]{2,0,1:T(2,128)S(1)}, f32[2,3,256]{2,0,1:T(2,128)}, u32[]{:S(2)}) copy-start(f32[2,3,256]{2,0,1:T(2,128)} %param.11) | copy-start | bytes 18436
  2.5 4.4 %collective-permute-start = (f32[32,256]{1,0:T(8,128)S(1)}, f32[32,256]{1,0:T(8,128)S(1)}, u32[]{:S(2)}, u32[]{:S(2)}) collective-permute-start(f32[32,256]{1,0:T(8,128)S(1)} %get-tuple-element.26.refs_4_), channel_id=1, source_target_pairs={{0,1},{1,0},{2,3},{3,2},{4,5},{5,4},{6,7},{7,6},{8,9},{9,8},{10,11... | collective-permute-start | bytes 98312 | tf_op jit(solution)/shard_map/ppermute | solution.py:553
  7.0 7.7 %collective-permute-start.1 = (f32[32,512]{1,0:T(8,128)S(1)}, f32[32,512]{1,0:T(8,128)S(1)}, u32[]{:S(2)}, u32[]{:S(2)}) collective-permute-start(f32[32,512]{1,0:T(8,128)S(1)} %pad_maximum_fusion.refs_2_.middle), channel_id=1, source_target_pairs={{0,2},{1,31},{2,4},{3,1},{4,6},{5,3},{6,8},{7,5},{8,10},{9,7},{10,... | collective-permute-start | bytes 196616 | tf_op jit(solution)/shard_map/ppermute | solution.py:555
  14.7 2.2 %collective-permute-start.2 = (f32[32,512]{1,0:T(8,128)S(1)}, f32[32,512]{1,0:T(8,128)S(1)}, u32[]{:S(2)}, u32[]{:S(2)}) collective-permute-start(f32[32,512]{1,0:T(8,128)S(1)} %collective-permute-done.1.refs_1_), channel_id=1, source_target_pairs={{0,1},{1,0},{2,3},{3,2},{4,5},{5,4},{6,7},{7,6},{8,9},{9,8},{10,11... | collective-permute-start | bytes 196616 | tf_op jit(solution)/shard_map/ppermute | solution.py:580
  22.4 6.7 %collective-permute-start.3 = (f32[8,512]{1,0:T(8,128)S(1)}, f32[8,512]{1,0:T(8,128)S(1)}, u32[]{:S(2)}, u32[]{:S(2)}) collective-permute-start(f32[8,512]{1,0:T(8,128)S(1)} %get-tuple-element.43.along), channel_id=1, source_target_pairs={{1,32},{3,34},{5,36},{7,38},{9,40},{11,42},{13,44},{15,46},{17,48}... | collective-permute-start | bytes 49160 | tf_op jit(solution)/shard_map/ppermute | solution.py:621
  29.8 16.1 %all-to-all-start = ((f32[32,1,128]{2,1,0:T(1,128)}), f32[32,1,128]{2,1,0:T(1,128)S(1)}, u32[]{:S(2)}, u32[]{:S(2)}) async-start(f32[32,1,128]{2,1,0:T(1,128)} %bitcast.5), calls=%async_computation | async-start | bytes 32768 | tf_op jit(solution)/shard_map/all_to_all | solution.py:646
  36.6 1.3 %collective-permute-start.4 = (f32[8,256]{1,0:T(8,128)S(1)}, f32[8,256]{1,0:T(8,128)S(1)}, u32[]{:S(2)}, u32[]{:S(2)}) collective-permute-start(f32[8,256]{1,0:T(8,128)S(1)} %get-tuple-element.46), channel_id=1, source_target_pairs={{0,1},{1,0},{2,3},{3,2},{4,5},{5,4},{6,7},{7,6},{8,9},{9,8},{10,11... | collective-permute-start | bytes 24584 | tf_op jit(solution)/shard_map/ppermute | solution.py:645

commit v3 on v2

--- a/solution.py
+++ b/solution.py
@@ -94,8 +94,20 @@
     return jnp.concatenate([both, both], axis=0)
 
 
-def prepare_kernel(packed, positions, out, site_of_slot):
-    slots = packed[64:66, :]
+def prepare_kernel(
+    neighbours_hbm, ghost_hbm, positions_hbm, out, site_of_slot, neighbours, ghost_slots, positions, arrived
+):
+    copies = [
+        pltpu.make_async_copy(source, target, arrived.at[number])
+        for number, (source, target) in enumerate(
+            ((ghost_hbm, ghost_slots), (neighbours_hbm, neighbours), (positions_hbm, positions))
+        )
+    ]
+    for copy in copies:
+        copy.start()
+    for copy in copies:
+        copy.wait()
+    slots = ghost_slots[...]
     inverse = jnp.zeros((8, 2 * LAYER), F32)
     for layer in range(NZL):
         hit = (jnp.broadcast_to(slots[layer : layer + 1], (2 * LAYER, LAYER)) == iota((2 * LAYER, LAYER), 0))
@@ -118,7 +130,7 @@
         )
         for half in range(2)
     ]
-    listed = packed[0:64, :].astype(F32)
+    listed = neighbours[...].astype(F32)
     turned = jnp.concatenate([listed, jnp.zeros((64, LAYER), F32)], axis=0).T
     site = iota((32, LAYER), 1)
     row = iota((32, LAYER), 0)
@@ -166,22 +178,38 @@
 SQUARE, HIDDEN, MESSAGE, OUTPUT = range(4)
 
 
-def weights_kernel(squares, radials, turned, straight, radial, radial_turned, energy):
+def weights_kernel(
+    w_square,
+    w_hidden,
+    w_message,
+    w_output,
+    w_radial1,
+    w_radial2,
+    w_energy,
+    turned,
+    straight,
+    radial,
+    radial_turned,
+    energy,
+    squares,
+    radials,
+    column,
+    arrived,
+):
+    moves = [(ref, squares.at[number]) for number, ref in enumerate((w_square, w_hidden, w_message, w_output))]
+    moves += [(w_radial1, radials.at[0]), (w_radial2, radials.at[1]), (w_energy, column)]
+    copies = [pltpu.make_async_copy(*move, arrived.at[number]) for number, move in enumerate(moves)]
+    for copy in copies:
+        copy.start()
+    for copy in copies:
+        copy.wait()
     for number in range(4):
         turned[number] = stationary(squares[number].T)
         straight[number] = stationary(squares[number])
     for number in range(2):
         radial[number] = stationary(radials[number])
         radial_turned[number] = radial_stationary(radials[number])
-    energy[...] = jnp.broadcast_to(radials[2, 0:1], (CH, CH)).T
-
-
-def stacked(arrays):
-    shape = (len(arrays),) + arrays[0].shape
-    out = jnp.broadcast_to(arrays[-1][None], shape)
-    for number, array in enumerate(arrays[:-1]):
-        out = jnp.where(iota(shape, 0) == number, jnp.broadcast_to(array[None], shape), out)
-    return out
+    energy[...] = jnp.broadcast_to(column[...], (CH, CH)).T
 
 
 def forward_kernel(
@@ -279,25 +307,44 @@
     first, second = radial_turned[0], radial_turned[1]
     square_t, hidden_t, message_t = turned[SQUARE], turned[HIDDEN], turned[MESSAGE]
 
-    mix = jnp.dot(
-        first,
-        radial_moving(jnp.concatenate([summed[e] for e in range(10)], axis=1)),
-        preferred_element_type=F32,
-    )
-    mixed = mix + product(square_t, mix * mix)
-    act, act_slope = silu_parts(product(hidden_t, mixed))
-    sent_on = product(message_t, act)
-    for e in range(10):
-        here = slice(e * LAYER, (e + 1) * LAYER)
-        hidden[e] = act[:, here]
-        if 2 <= e <= 7:
-            radial_mix[e - 2] = mix[:, here]
-            hidden_slope[e - 2] = act_slope[:, here]
-        for number, (dx, dy) in enumerate(LATERALS):
-            part = sent_on[:, here]
-            if (dx, dy) != (0, 0):
-                part = take(part, shifted_site((CH, LAYER), dx, dy))
-            message[number, e] = part
+    held = {}
+
+    def node_mix(pair):
+        mix = jnp.dot(
+            first,
+            radial_moving(jnp.concatenate([summed[2 * pair], summed[2 * pair + 1]], axis=1)),
+            preferred_element_type=F32,
+        )
+        for k in range(2):
+            if 2 <= 2 * pair <= 6:
+                radial_mix[2 * pair + k - 2] = mix[:, k * LAYER : (k + 1) * LAYER]
+        held[pair] = mix, product(square_t, mix * mix)
+
+    def node_hidden(pair):
+        mix, mixed = held[pair]
+        held[pair] = product(hidden_t, mix + mixed)
+
+    def node_message(pair):
+        act, act_slope = silu_parts(held[pair])
+        for k in range(2):
+            hidden[2 * pair + k] = act[:, k * LAYER : (k + 1) * LAYER]
+            if 2 <= 2 * pair <= 6:
+                hidden_slope[2 * pair + k - 2] = act_slope[:, k * LAYER : (k + 1) * LAYER]
+        held[pair] = product(message_t, act)
+
+    def node_send(pair):
+        for k in range(2):
+            for number, (dx, dy) in enumerate(LATERALS):
+                part = held[pair][:, k * LAYER : (k + 1) * LAYER]
+                if (dx, dy) != (0, 0):
+                    part = take(part, shifted_site((CH, LAYER), dx, dy))
+                message[number, 2 * pair + k] = part
+
+    stages = (node_mix, node_hidden, node_message, node_send)
+    for step in range(5 + len(stages) - 1):
+        for number, stage in enumerate(stages):
+            if 0 <= step - number < 5:
+                stage(step - number)
 
     output_t, output_n = turned[OUTPUT], straight[OUTPUT]
 
@@ -314,16 +361,28 @@
             )
             number = LATERAL_OF[(dx, dy)]
             total = total + radial * jnp.concatenate([message[number, e + dz], message[number, e + 1 + dz]], axis=1)
-        return total
-
-    total = jnp.concatenate([readout(pair) for pair in range(4)], axis=1)
-    weight = jnp.concatenate([w_energy[...]] * 8, axis=1)
-    act, act_slope = silu_parts(product(output_t, total))
-    grad = product(output_n, weight * act_slope)
-    for a in range(8):
-        grad_out[a] = grad[:, a * LAYER : (a + 1) * LAYER]
-    own = slice(2 * LAYER, 6 * LAYER)
-    energy = jnp.sum(weight[:, own] * act[:, own], axis=0, keepdims=True)
+        held[pair] = total
+
+    weight = jnp.concatenate([w_energy[...]] * 2, axis=1)
+    energies = []
+
+    def readout_energy(pair):
+        act, act_slope = silu_parts(product(output_t, held[pair]))
+        if 1 <= pair <= 2:
+            energies.append(jnp.sum(weight * act, axis=0, keepdims=True))
+        held[pair] = weight * act_slope
+
+    def readout_grad(pair):
+        grad = product(output_n, held[pair])
+        grad_out[2 * pair] = grad[:, :LAYER]
+        grad_out[2 * pair + 1] = grad[:, LAYER:]
+
+    stages = (readout, readout_energy, readout_grad)
+    for step in range(4 + len(stages) - 1):
+        for number, stage in enumerate(stages):
+            if 0 <= step - number < 4:
+                stage(step - number)
+    energy = energies[0] + energies[1]
 
     along[0:3] = jnp.where(even, middle[26:29, :], middle[29:32, :])
     along[3:4] = jnp.where(iota((1, 4 * LAYER), 1) == 0, jnp.sum(energy), 0.0)
@@ -512,6 +571,14 @@
     return pl.BlockSpec(memory_space=pltpu.VMEM)
 
 
+def hbm():
+    return pl.BlockSpec(memory_space=pltpu.HBM)
+
+
+def stay(array):
+    return pltpu.with_memory_space_constraint(array, pltpu.HBM)
+
+
 def smem():
     return pl.BlockSpec(memory_space=pltpu.SMEM)
 
@@ -538,17 +605,24 @@
     parity_arg = parity.astype(I32).reshape(1)
 
     small = pltpu.CompilerParams(vmem_limit_bytes=4 * 1024 * 1024)
-    packed = jnp.concatenate([neighbours.reshape(64, LAYER), ghost_slots], axis=0)
     prepared, site_of_slot = pl.pallas_call(
         prepare_kernel,
         out_shape=(
             jax.ShapeDtypeStruct((ROWS, 2 * LAYER), F32),
             jax.ShapeDtypeStruct((8, 2 * LAYER), I32),
         ),
-        in_specs=[vmem()] * 2,
+        in_specs=[hbm()] * 3,
         out_specs=(vmem(), vmem()),
+        scratch_shapes=[
+            pltpu.VMEM((64, LAYER), I32),
+            pltpu.VMEM((2, LAYER), I32),
+            pltpu.VMEM((3, 2, 2 * LAYER), F32),
+            pltpu.SemaphoreType.DMA((3,)),
+        ],
         compiler_params=small,
-    )(packed, positions.transpose(1, 0, 2))
+    )(
+        stay(neighbours.reshape(64, LAYER)), stay(ghost_slots), stay(positions.transpose(1, 0, 2))
+    )
 
     mate = lax.ppermute(prepared, "slab", [(i, i ^ 1) for i in range(slabs)])
     middle = jnp.concatenate([jnp.where(even, prepared, mate), jnp.where(even, mate, prepared)], axis=1)
@@ -567,14 +641,17 @@
             jax.ShapeDtypeStruct((2, CH, 4 * NB), BF16),
             whole(CH, CH),
         ),
-        in_specs=[vmem()] * 2,
+        in_specs=[hbm()] * 7,
         out_specs=tuple(vmem() for _ in range(5)),
+        scratch_shapes=[
+            pltpu.VMEM((4, CH, CH), F32),
+            pltpu.VMEM((2, NB, CH), F32),
+            pltpu.VMEM((1, CH), F32),
+            pltpu.SemaphoreType.DMA((7,)),
+        ],
         compiler_params=small,
         cost_estimate=pl.CostEstimate(flops=10**8, bytes_accessed=1 << 22, transcendentals=0),
-    )(
-        stacked([w_square, w_hidden, w_message, w_output]),
-        stacked([w_radial1, w_radial2, jnp.broadcast_to(w_energy[None], (NB, CH))]),
-    )
+    )(*map(stay, (w_square, w_hidden, w_message, w_output, w_radial1, w_radial2, w_energy.reshape(1, CH))))
 
     far, turned, straight = lax.optimization_barrier((far, turned, straight))
     traded = lax.ppermute(far, "slab", [(i, i ^ 1) for i in range(slabs)])

time: 47.2 us -> 46.3 us (0.981)
  other arithmetic: 2.65 us -> 0.01 us
  Pallas kernels: 12.2 us -> 13.8 us
  local copies, waits for them, and re-layouts: 0.69 us -> 0 us
  waiting for transfers between devices: 9.48 us -> 10.1 us
    select_n x2 -> x0, other arithmetic: 1.84 us -> none  [stacked(): jnp.where(iota(shape, 0) == number, jnp.broadcast_to(array[None], shape),...]
    pallas_call x1, Pallas kernels: 0.34 us -> 1.34 us  [local(): pl.pallas_call(weights_kernel, out_shape=(jax.ShapeDtypeStruct((4, 2 * CH...]
    ppermute x1, waiting for transfers between devices: 0.01 us -> 0.86 us  [local(): mate = lax.ppermute(prepared, 'slab', [(i, i ^ 1) for i in range(slabs)])]
    pallas_call x1, Pallas kernels: 0.39 us -> 1.19 us  [local(): pl.pallas_call(prepare_kernel, out_shape=(jax.ShapeDtypeStruct((ROWS, 2 *...]
    concatenate x1 -> x0, other arithmetic: 0.78 us -> none  [local(): jnp.concatenate([neighbours.reshape(64, LAYER), ghost_slots], axis=0)]
    unnamed x2 -> x0, local copies, waits for them, and re-layouts: 0.69 us -> none
  transfers between devices with their start and end apart: 6 -> 6, of which waited for: 4 -> 4; matrix products, arithmetic and copies ran while one was open for 4% -> 0% of each run, Pallas kernels for 10% -> 12%
where the time goes in v3:
time: 46.3 us; the launch traced here: 46.1 us
  starting transfers between devices  20.7 us (45%)
  Pallas kernels  13.8 us (30%)
  waiting for transfers between devices  10.1 us (22%)
  between operations  1.35 us (3%)
    all_to_all x1, waiting for transfers between devices, local(): lax.all_to_all(table.reshape(slabs, 1, LAYER), 'slab', 0, 0, tiled=False)  8.09 us
    all_to_all x1, starting transfers between devices, local(): lax.all_to_all(table.reshape(slabs, 1, LAYER), 'slab', 0, 0, tiled=False)  6.72 us
    ppermute x1, starting transfers between devices, local(): lax.ppermute(middle, 'slab', [(i, (i + 2) % slabs) if i % 2 == 0 else (i,...  6.38 us
    pallas_call x1, Pallas kernels, local(): pl.pallas_call(lambda *refs: forward_kernel(slabs * NZL * LATTICE, *refs)...  5.44 us
    pallas_call x1, Pallas kernels, local(): pl.pallas_call(backward_kernel, out_shape=whole(8, 4 * LAYER), in_specs=[...  4.18 us
    ppermute x1, starting transfers between devices, local(): mate = lax.ppermute(prepared, 'slab', [(i, i ^ 1) for i in range(slabs)])  3.33 us
    ppermute x1, starting transfers between devices, local(): path = lax.ppermute(along, ('image', 'slab'), hops)  2.46 us
    ppermute x1, starting transfers between devices, local(): traded = lax.ppermute(far, 'slab', [(i, i ^ 1) for i in range(slabs)])  1.53 us
  transfers between devices with their start and end apart: 6, of which 4 were waited for; matrix products, arithmetic and copies ran while one was open for 0% of the time, Pallas kernels for 12%

profile of v3, /device:TPU:1, one launch (start us, length us, event | category | flops | bytes accessed | tf_op | source)
XLA Modules:
  0.0 46.1 jit_solution(11740590445086822651)
XLA Ops:
  0.6 1.2 %shard_map.122 = (f32[32,256]{1,0:T(8,128)S(1)}, s32[8,256]{1,0:T(8,128)S(1)}) custom-call(s32[64,128]{1,0:T(8,128)} %bitcast.11, s32[2,128]{1,0:T(2,128)} %ghost_hbm.1, f32[3,2,256]{2,1,0:T(2,128)} %bitcast.12), custom_call_target="tpu_custom_call" | custom-call | tf_op jit(solution)/shard_map/pallas_call | solution.py:608
  1.8 3.3 %collective-permute-start = (f32[32,256]{1,0:T(8,128)S(1)}, f32[32,256]{1,0:T(8,128)S(1)}, u32[]{:S(2)}, u32[]{:S(2)}) collective-permute-start(f32[32,256]{1,0:T(8,128)S(1)} %get-tuple-element.26.refs_4_), channel_id=1, source_target_pairs={{0,1},{1,0},{2,3},{3,2},{4,5},{5,4},{6,7},{7,6},{8,9},{9,8},{10,11... | collective-permute-start | bytes 98312 | tf_op jit(solution)/shard_map/ppermute | solution.py:627
  5.2 0.9 %collective-permute-done = f32[32,256]{1,0:T(8,128)S(1)} collective-permute-done((f32[32,256]{1,0:T(8,128)S(1)}, f32[32,256]{1,0:T(8,128)S(1)}, u32[]{:S(2)}, u32[]{:S(2)}) %collective-permute-start) | collective-permute-done | bytes 32800 | tf_op jit(solution)/shard_map/ppermute | solution.py:627
  6.0 6.4 %collective-permute-start.1 = (f32[32,512]{1,0:T(8,128)S(1)}, f32[32,512]{1,0:T(8,128)S(1)}, u32[]{:S(2)}, u32[]{:S(2)}) collective-permute-start(f32[32,512]{1,0:T(8,128)S(1)} %pad_maximum_fusion.refs_2_.middle), channel_id=1, source_target_pairs={{0,2},{1,31},{2,4},{3,1},{4,6},{5,3},{6,8},{7,5},{8,10},{9,7},{10,... | collective-permute-start | bytes 196616 | tf_op jit(solution)/shard_map/ppermute | solution.py:629
  12.4 1.3 %shard_map.123 = (bf16[4,256,256]{2,1,0:T(8,128)(2,1)S(1)}, bf16[4,256,256]{2,1,0:T(8,128)(2,1)S(1)}, bf16[2,16,256]{2,1,0:T(8,128)(2,1)S(1)}, bf16[2,128,32]{2,1,0:T(8,128)(2,1)S(1)}, f32[128,128]{1,0:T(8,128)S(1)}) custom-call(f32[128,128]{1,0:T(8,128)} %w_square.1, f32[128,128]{1,0:T(8,128)} %w_hidden.1, f32[128,128]{1,0:T(8,128)} %w_message.1, ...), custom_call_target="tpu_custom_call" | custom-call | flops 100000000 | bytes 4194304 | tf_op jit(solution)/shard_map/pallas_call | solution.py:635
  13.8 0.0 collective-permute-done.1.refs_1_
  13.8 1.5 %collective-permute-start.2 = (f32[32,512]{1,0:T(8,128)S(1)}, f32[32,512]{1,0:T(8,128)S(1)}, u32[]{:S(2)}, u32[]{:S(2)}) collective-permute-start(f32[32,512]{1,0:T(8,128)S(1)} %collective-permute-done.1.refs_1_), channel_id=1, source_target_pairs={{0,1},{1,0},{2,3},{3,2},{4,5},{5,4},{6,7},{7,6},{8,9},{9,8},{10,11... | collective-permute-start | bytes 196616 | tf_op jit(solution)/shard_map/ppermute | solution.py:657
  15.3 0.9 %collective-permute-done.2.refs_3_ = f32[32,512]{1,0:T(8,128)S(1)} collective-permute-done((f32[32,512]{1,0:T(8,128)S(1)}, f32[32,512]{1,0:T(8,128)S(1)}, u32[]{:S(2)}, u32[]{:S(2)}) %collective-permute-start.2) | collective-permute-done | bytes 65568 | tf_op jit(solution)/shard_map/ppermute | solution.py:657
  16.2 5.4 %shard_map.124 = (f32[8,512]{1,0:T(8,128)S(1)}, f32[4,3,32,128]{3,2,1,0:T(8,128)S(1)}, f32[4,32,128]{2,1,0:T(8,128)S(1)}, f32[6,256,128]{2,1,0:T(8,128)S(1)}, f3...) custom-call(s32[1]{0:T(128)} %bitcast.1.refs_0_.parity.refs_1_, ...), custom_call_target="tpu_custom_call" | custom-call | tf_op jit(solution)/shard_map/pallas_call | solution.py:659
  21.6 2.5 %collective-permute-start.3 = (f32[8,512]{1,0:T(8,128)S(1)}, f32[8,512]{1,0:T(8,128)S(1)}, u32[]{:S(2)}, u32[]{:S(2)}) collective-permute-start(f32[8,512]{1,0:T(8,128)S(1)} %get-tuple-element.43.along), channel_id=1, source_target_pairs={{1,32},{3,34},{5,36},{7,38},{9,40},{11,42},{13,44},{15,46},{17,48}... | collective-permute-start | bytes 49160 | tf_op jit(solution)/shard_map/ppermute | solution.py:698
  24.1 4.2 %shard_map.125.forces = f32[8,512]{1,0:T(8,128)S(1)} custom-call(f32[4,3,32,128]{3,2,1,0:T(8,128)S(1)} %get-tuple-element.34.reach, f32[4,32,128]{2,1,0:T(8,128)S(1)} %get-tuple-element.35.inverse_radius, f32[6,256,128]{2,1,0:T(8,128)S(1)} %get-tuple-element.36.slope, f32[6,128,128]{2,1,0:T(8,128)S(1)} %get-tuple-element.37.radial_mix, ...), custom_call_target="tpu_custom_call" | custom-call | flops 4000000000 | bytes 4194304 | tf_op jit(solution)/shard_map/pallas_call | solution.py:700
  28.3 0.0 collective-permute-done.3.path
  28.3 0.7 %shard_map.126 = (f32[32,128]{1,0:T(8,128)}, f32[8,256]{1,0:T(8,128)S(1)}, f32[8,256]{1,0:T(8,128)S(1)}) custom-call(s32[1]{0:T(128)} %bitcast.1.refs_0_.parity.refs_1_, f32[32,512]{1,0:T(8,128)S(1)} %pad_maximum_fusion.refs_2_.middle, f32[8,512]{1,0:T(8,128)S(1)} %shard_map.125.forces, f32[8,512]{1,0:T(8,128)S(1)} %get-tuple-element.43.along, ...), custom_call_target="tpu_custom_call" | custom-call | tf_op jit(solution)/shard_map/pallas_call | solution.py:714
  29.0 6.7 %all-to-all-start = ((f32[32,1,128]{2,1,0:T(1,128)}), f32[32,1,128]{2,1,0:T(1,128)S(1)}, u32[]{:S(2)}, u32[]{:S(2)}) async-start(f32[32,1,128]{2,1,0:T(1,128)} %bitcast.6), calls=%async_computation | async-start | bytes 32768 | tf_op jit(solution)/shard_map/all_to_all | solution.py:723
  35.8 0.3 collective-permute-start.4
  36.7 0.3 collective-permute-done.4.refs_6_
  37.0 8.1 %all-to-all-done = f32[32,1,128]{2,1,0:T(1,128)S(1)} async-done(((f32[32,1,128]{2,1,0:T(1,128)}), f32[32,1,128]{2,1,0:T(1,128)S(1)}, u32[]{:S(2)}, u32[]{:S(2)}) %all-to-all-start) | async-done | bytes 16416 | tf_op jit(solution)/shard_map/all_to_all | solution.py:723
  45.1 0.9 %shard_map.127 = (f32[3,2,256]{2,1,0:T(2,128)}, f32[2]{0:T(128)}) custom-call(s32[1]{0:T(128)} %bitcast.refs_0_, s32[1]{0:T(128)} %bitcast.1.refs_0_.parity.refs_1_, s32[1]{0:T(128)S(6)} %copy.14.refs_2_, f32[32,128]{1,0:T(8,128)S(1)} %bitcast.10, f32[32,256]{1,0:T(8,128)S(1)} %get-tuple-element.26.refs_4_, f32[8,256]{1,0:T(8,128)S(1)} %get-tuple-element.45.refs_5_, ...), custom_call_target="tpu_custom_call" | custom-call | tf_op jit(solution)/shard_map/pallas_call | solution.py:725
  (2 shorter events, 0.0 us)
Async XLA Ops:
  1.8 4.2 %collective-permute-start = (f32[32,256]{1,0:T(8,128)S(1)}, f32[32,256]{1,0:T(8,128)S(1)}, u32[]{:S(2)}, u32[]{:S(2)}) collective-permute-start(f32[32,256]{1,0:T(8,128)S(1)} %get-tuple-element.26.refs_4_), channel_id=1, source_target_pairs={{0,1},{1,0},{2,3},{3,2},{4,5},{5,4},{6,7},{7,6},{8,9},{9,8},{10,11... | collective-permute-start | bytes 98312 | tf_op jit(solution)/shard_map/ppermute | solution.py:627
  6.0 7.7 %collective-permute-start.1 = (f32[32,512]{1,0:T(8,128)S(1)}, f32[32,512]{1,0:T(8,128)S(1)}, u32[]{:S(2)}, u32[]{:S(2)}) collective-permute-start(f32[32,512]{1,0:T(8,128)S(1)} %pad_maximum_fusion.refs_2_.middle), channel_id=1, source_target_pairs={{0,2},{1,31},{2,4},{3,1},{4,6},{5,3},{6,8},{7,5},{8,10},{9,7},{10,... | collective-permute-start | bytes 196616 | tf_op jit(solution)/shard_map/ppermute | solution.py:629
  13.8 2.4 %collective-permute-start.2 = (f32[32,512]{1,0:T(8,128)S(1)}, f32[32,512]{1,0:T(8,128)S(1)}, u32[]{:S(2)}, u32[]{:S(2)}) collective-permute-start(f32[32,512]{1,0:T(8,128)S(1)} %collective-permute-done.1.refs_1_), channel_id=1, source_target_pairs={{0,1},{1,0},{2,3},{3,2},{4,5},{5,4},{6,7},{7,6},{8,9},{9,8},{10,11... | collective-permute-start | bytes 196616 | tf_op jit(solution)/shard_map/ppermute | solution.py:657
  21.6 6.7 %collective-permute-start.3 = (f32[8,512]{1,0:T(8,128)S(1)}, f32[8,512]{1,0:T(8,128)S(1)}, u32[]{:S(2)}, u32[]{:S(2)}) collective-permute-start(f32[8,512]{1,0:T(8,128)S(1)} %get-tuple-element.43.along), channel_id=1, source_target_pairs={{1,32},{3,34},{5,36},{7,38},{9,40},{11,42},{13,44},{15,46},{17,48}... | collective-permute-start | bytes 49160 | tf_op jit(solution)/shard_map/ppermute | solution.py:698
  29.0 16.1 %all-to-all-start = ((f32[32,1,128]{2,1,0:T(1,128)}), f32[32,1,128]{2,1,0:T(1,128)S(1)}, u32[]{:S(2)}, u32[]{:S(2)}) async-start(f32[32,1,128]{2,1,0:T(1,128)} %bitcast.6), calls=%async_computation | async-start | bytes 32768 | tf_op jit(solution)/shard_map/all_to_all | solution.py:723
  35.8 1.3 %collective-permute-start.4 = (f32[8,256]{1,0:T(8,128)S(1)}, f32[8,256]{1,0:T(8,128)S(1)}, u32[]{:S(2)}, u32[]{:S(2)}) collective-permute-start(f32[8,256]{1,0:T(8,128)S(1)} %get-tuple-element.46), channel_id=1, source_target_pairs={{0,1},{1,0},{2,3},{3,2},{4,5},{5,4},{6,7},{7,6},{8,9},{9,8},{10,11... | collective-permute-start | bytes 24584 | tf_op jit(solution)/shard_map/ppermute | solution.py:722

commit v4 on v3

--- a/solution.py
+++ b/solution.py
@@ -214,7 +214,7 @@
 
 def forward_kernel(
     cell_z,
-    parity,
+    side,
     far,
     middle,
     traded,
@@ -234,15 +234,18 @@
     coords,
     summed,
     hidden,
+    outer,
 ):
-    even = parity[0] == 0
+    even = (side[0] & 1) == 0
+    place = side[0] >> 1
+    outer[place] = far[...]
+    outer[1 - place] = traded[...]
 
     def level_rows(level, first, last):
         here = slice(level % 4 * LAYER, (level % 4 + 1) * LAYER)
         if 4 <= level < 8:
             return middle[first:last, here]
-        mine, other = far[first:last, here], traded[first:last, here]
-        return jnp.where(even, mine, other) if level < 4 else jnp.where(even, other, mine)
+        return outer[0 if level < 4 else 1, first:last, here]
 
     for level in range(12):
         both = level_rows(level, 24, 32)
@@ -626,9 +629,15 @@
 
     mate = lax.ppermute(prepared, "slab", [(i, i ^ 1) for i in range(slabs)])
     middle = jnp.concatenate([jnp.where(even, prepared, mate), jnp.where(even, mate, prepared)], axis=1)
-    far = lax.ppermute(
-        middle, "slab", [(i, (i + 2) % slabs) if i % 2 == 0 else (i, (i - 2) % slabs) for i in range(slabs)]
-    )
+    pairs = slabs // 2
+    partners = []
+    for i in range(slabs):
+        p = i // 2
+        other = p ^ 1 if i % 2 == 0 else (p + 1 if p % 2 else p - 1) % pairs
+        partners.append((i, 2 * other + i % 2))
+    far = lax.ppermute(middle, "slab", partners)
+    side = ((slab & 1) | ((((slab >> 1) + slab + 1) & 1) << 1)).astype(I32).reshape(1)
+
     def whole(*extents):
         return jax.ShapeDtypeStruct(extents, F32)
 
@@ -675,10 +684,11 @@
             pltpu.VMEM((12, 8, LAYER), F32),
             pltpu.VMEM((10, NB, LAYER), F32),
             pltpu.VMEM((10, CH, LAYER), F32),
+            pltpu.VMEM((2, ROWS, 4 * LAYER), F32),
         ],
         compiler_params=pltpu.CompilerParams(vmem_limit_bytes=20 * 1024 * 1024),
     )(
-        parity_arg,
+        side,
         far,
         middle,
         traded,

time: 46.3 us -> 46.1 us (level)
  starting transfers between devices: 20.7 us -> 19.8 us
  waiting for transfers between devices: 10.1 us -> 10.8 us
    ppermute x1, starting transfers between devices: 1.53 us -> 0.01 us  [local(): traded = lax.ppermute(far, 'slab', [(i, i ^ 1) for i in range(slabs)])]
    all_to_all x1, starting transfers between devices: 6.72 us -> 7.5 us  [local(): lax.all_to_all(table.reshape(slabs, 1, LAYER), 'slab', 0, 0, tiled=False)]
  transfers between devices with their start and end apart: 6 -> 6, of which waited for: 4 -> 5; matrix products, arithmetic and copies ran while one was open for 0% -> 0% of each run, Pallas kernels for 12% -> 12%
where the time goes in v4:
time: 46.1 us; the launch traced here: 45.8 us
  starting transfers between devices  19.8 us (43%)
  Pallas kernels  13.8 us (30%)
  waiting for transfers between devices  10.8 us (23%)
  between operations  1.34 us (3%)
    all_to_all x1, waiting for transfers between devices, local(): lax.all_to_all(table.reshape(slabs, 1, LAYER), 'slab', 0, 0, tiled=False)  8.09 us
    all_to_all x1, starting transfers between devices, local(): lax.all_to_all(table.reshape(slabs, 1, LAYER), 'slab', 0, 0, tiled=False)  7.5 us
    ppermute x1, starting transfers between devices, local(): far = lax.ppermute(middle, 'slab', partners)  6.39 us
    pallas_call x1, Pallas kernels, local(): pl.pallas_call(lambda *refs: forward_kernel(slabs * NZL * LATTICE, *refs)...  5.44 us
    pallas_call x1, Pallas kernels, local(): pl.pallas_call(backward_kernel, out_shape=whole(8, 4 * LAYER), in_specs=[...  4.18 us
    ppermute x1, starting transfers between devices, local(): mate = lax.ppermute(prepared, 'slab', [(i, i ^ 1) for i in range(slabs)])  3.33 us
    ppermute x1, starting transfers between devices, local(): path = lax.ppermute(along, ('image', 'slab'), hops)  2.26 us
    pallas_call x1, Pallas kernels, local(): pl.pallas_call(weights_kernel, out_shape=(jax.ShapeDtypeStruct((4, 2 * CH...  1.34 us
  transfers between devices with their start and end apart: 6, of which 5 were waited for; matrix products, arithmetic and copies ran while one was open for 0% of the time, Pallas kernels for 12%

profile of v4, /device:TPU:1, one launch (start us, length us, event | category | flops | bytes accessed | tf_op | source)
XLA Modules:
  0.0 45.8 jit_solution(9825886167949712896)
XLA Ops:
  0.6 1.2 %shard_map.122 = (f32[32,256]{1,0:T(8,128)S(1)}, s32[8,256]{1,0:T(8,128)S(1)}) custom-call(s32[64,128]{1,0:T(8,128)} %bitcast.12, s32[2,128]{1,0:T(2,128)} %ghost_hbm.1, f32[3,2,256]{2,1,0:T(2,128)} %bitcast.13), custom_call_target="tpu_custom_call" | custom-call | tf_op jit(solution)/shard_map/pallas_call | solution.py:611
  1.8 3.3 %collective-permute-start = (f32[32,256]{1,0:T(8,128)S(1)}, f32[32,256]{1,0:T(8,128)S(1)}, u32[]{:S(2)}, u32[]{:S(2)}) collective-permute-start(f32[32,256]{1,0:T(8,128)S(1)} %get-tuple-element.26.refs_4_), channel_id=1, source_target_pairs={{0,1},{1,0},{2,3},{3,2},{4,5},{5,4},{6,7},{7,6},{8,9},{9,8},{10,11... | collective-permute-start | bytes 98312 | tf_op jit(solution)/shard_map/ppermute | solution.py:630
  5.2 0.9 %collective-permute-done = f32[32,256]{1,0:T(8,128)S(1)} collective-permute-done((f32[32,256]{1,0:T(8,128)S(1)}, f32[32,256]{1,0:T(8,128)S(1)}, u32[]{:S(2)}, u32[]{:S(2)}) %collective-permute-start) | collective-permute-done | bytes 32800 | tf_op jit(solution)/shard_map/ppermute | solution.py:630
  6.0 6.4 %collective-permute-start.1 = (f32[32,512]{1,0:T(8,128)S(1)}, f32[32,512]{1,0:T(8,128)S(1)}, u32[]{:S(2)}, u32[]{:S(2)}) collective-permute-start(f32[32,512]{1,0:T(8,128)S(1)} %pad_maximum_fusion.refs_2_.middle), channel_id=1, source_target_pairs={{0,2},{1,31},{2,0},{3,5},{4,6},{5,3},{6,4},{7,9},{8,10},{9,7},{10,... | collective-permute-start | bytes 196616 | tf_op jit(solution)/shard_map/ppermute | solution.py:638
  12.4 1.3 %shard_map.123 = (bf16[4,256,256]{2,1,0:T(8,128)(2,1)S(1)}, bf16[4,256,256]{2,1,0:T(8,128)(2,1)S(1)}, bf16[2,16,256]{2,1,0:T(8,128)(2,1)S(1)}, bf16[2,128,32]{2,1,0:T(8,128)(2,1)S(1)}, f32[128,128]{1,0:T(8,128)S(1)}) custom-call(f32[128,128]{1,0:T(8,128)} %w_square.1, f32[128,128]{1,0:T(8,128)} %w_hidden.1, f32[128,128]{1,0:T(8,128)} %w_message.1, ...), custom_call_target="tpu_custom_call" | custom-call | flops 100000000 | bytes 4194304 | tf_op jit(solution)/shard_map/pallas_call | solution.py:644
  13.8 0.3 collective-permute-done.1.refs_1_
  14.1 0.0 collective-permute-start.2
  14.1 1.3 %collective-permute-done.2.refs_3_ = f32[32,512]{1,0:T(8,128)S(1)} collective-permute-done((f32[32,512]{1,0:T(8,128)S(1)}, f32[32,512]{1,0:T(8,128)S(1)}, u32[]{:S(2)}, u32[]{:S(2)}) %collective-permute-start.2) | collective-permute-done | bytes 65568 | tf_op jit(solution)/shard_map/ppermute | solution.py:666
  15.3 5.4 %shard_map.124 = (f32[8,512]{1,0:T(8,128)S(1)}, f32[4,3,32,128]{3,2,1,0:T(8,128)S(1)}, f32[4,32,128]{2,1,0:T(8,128)S(1)}, f32[6,256,128]{2,1,0:T(8,128)S(1)}, f3...) custom-call(s32[1]{0:T(128)} %bitcast.4.refs_0_, ...), custom_call_target="tpu_custom_call" | custom-call | tf_op jit(solution)/shard_map/pallas_call | solution.py:668
  20.8 2.3 %collective-permute-start.3 = (f32[8,512]{1,0:T(8,128)S(1)}, f32[8,512]{1,0:T(8,128)S(1)}, u32[]{:S(2)}, u32[]{:S(2)}) collective-permute-start(f32[8,512]{1,0:T(8,128)S(1)} %get-tuple-element.43.along), channel_id=1, source_target_pairs={{1,32},{3,34},{5,36},{7,38},{9,40},{11,42},{13,44},{15,46},{17,48}... | collective-permute-start | bytes 49160 | tf_op jit(solution)/shard_map/ppermute | solution.py:708
  23.0 4.2 %shard_map.125.forces = f32[8,512]{1,0:T(8,128)S(1)} custom-call(f32[4,3,32,128]{3,2,1,0:T(8,128)S(1)} %get-tuple-element.34.reach, f32[4,32,128]{2,1,0:T(8,128)S(1)} %get-tuple-element.35.inverse_radius, f32[6,256,128]{2,1,0:T(8,128)S(1)} %get-tuple-element.36.slope, f32[6,128,128]{2,1,0:T(8,128)S(1)} %get-tuple-element.37.radial_mix, ...), custom_call_target="tpu_custom_call" | custom-call | flops 4000000000 | bytes 4194304 | tf_op jit(solution)/shard_map/pallas_call | solution.py:710
  27.2 0.0 collective-permute-done.3.path
  27.2 0.7 %shard_map.126 = (f32[32,128]{1,0:T(8,128)}, f32[8,256]{1,0:T(8,128)S(1)}, f32[8,256]{1,0:T(8,128)S(1)}) custom-call(s32[1]{0:T(128)} %bitcast.1.parity.refs_1_, f32[32,512]{1,0:T(8,128)S(1)} %pad_maximum_fusion.refs_2_.middle, f32[8,512]{1,0:T(8,128)S(1)} %shard_map.125.forces, f32[8,512]{1,0:T(8,128)S(1)} %get-tuple-element.43.along, ...), custom_call_target="tpu_custom_call" | custom-call | tf_op jit(solution)/shard_map/pallas_call | solution.py:724
  28.0 7.5 %all-to-all-start = ((f32[32,1,128]{2,1,0:T(1,128)}), f32[32,1,128]{2,1,0:T(1,128)S(1)}, u32[]{:S(2)}, u32[]{:S(2)}) async-start(f32[32,1,128]{2,1,0:T(1,128)} %bitcast.7), calls=%async_computation | async-start | bytes 32768 | tf_op jit(solution)/shard_map/all_to_all | solution.py:733
  35.5 0.3 collective-permute-start.4
  36.5 0.3 collective-permute-done.4.refs_6_
  36.7 8.1 %all-to-all-done = f32[32,1,128]{2,1,0:T(1,128)S(1)} async-done(((f32[32,1,128]{2,1,0:T(1,128)}), f32[32,1,128]{2,1,0:T(1,128)S(1)}, u32[]{:S(2)}, u32[]{:S(2)}) %all-to-all-start) | async-done | bytes 16416 | tf_op jit(solution)/shard_map/all_to_all | solution.py:733
  44.8 0.9 %shard_map.127 = (f32[3,2,256]{2,1,0:T(2,128)}, f32[2]{0:T(128)}) custom-call(s32[1]{0:T(128)} %bitcast.refs_0_, s32[1]{0:T(128)} %bitcast.1.parity.refs_1_, s32[1]{0:T(128)S(6)} %copy.14.refs_2_, f32[32,128]{1,0:T(8,128)S(1)} %bitcast.11, f32[32,256]{1,0:T(8,128)S(1)} %get-tuple-element.26.refs_4_, f32[8,256]{1,0:T(8,128)S(1)} %get-tuple-element.45.refs_5_, ...), custom_call_target="tpu_custom_call" | custom-call | tf_op jit(solution)/shard_map/pallas_call | solution.py:735
  (2 shorter events, 0.0 us)
Async XLA Ops:
  1.8 4.2 %collective-permute-start = (f32[32,256]{1,0:T(8,128)S(1)}, f32[32,256]{1,0:T(8,128)S(1)}, u32[]{:S(2)}, u32[]{:S(2)}) collective-permute-start(f32[32,256]{1,0:T(8,128)S(1)} %get-tuple-element.26.refs_4_), channel_id=1, source_target_pairs={{0,1},{1,0},{2,3},{3,2},{4,5},{5,4},{6,7},{7,6},{8,9},{9,8},{10,11... | collective-permute-start | bytes 98312 | tf_op jit(solution)/shard_map/ppermute | solution.py:630
  6.0 8.0 %collective-permute-start.1 = (f32[32,512]{1,0:T(8,128)S(1)}, f32[32,512]{1,0:T(8,128)S(1)}, u32[]{:S(2)}, u32[]{:S(2)}) collective-permute-start(f32[32,512]{1,0:T(8,128)S(1)} %pad_maximum_fusion.refs_2_.middle), channel_id=1, source_target_pairs={{0,2},{1,31},{2,0},{3,5},{4,6},{5,3},{6,4},{7,9},{8,10},{9,7},{10,... | collective-permute-start | bytes 196616 | tf_op jit(solution)/shard_map/ppermute | solution.py:638
  14.1 1.3 %collective-permute-start.2 = (f32[32,512]{1,0:T(8,128)S(1)}, f32[32,512]{1,0:T(8,128)S(1)}, u32[]{:S(2)}, u32[]{:S(2)}) collective-permute-start(f32[32,512]{1,0:T(8,128)S(1)} %collective-permute-done.1.refs_1_), channel_id=1, source_target_pairs={{0,1},{1,0},{2,3},{3,2},{4,5},{5,4},{6,7},{7,6},{8,9},{9,8},{10,11... | collective-permute-start | bytes 196616 | tf_op jit(solution)/shard_map/ppermute | solution.py:666
  20.8 6.5 %collective-permute-start.3 = (f32[8,512]{1,0:T(8,128)S(1)}, f32[8,512]{1,0:T(8,128)S(1)}, u32[]{:S(2)}, u32[]{:S(2)}) collective-permute-start(f32[8,512]{1,0:T(8,128)S(1)} %get-tuple-element.43.along), channel_id=1, source_target_pairs={{1,32},{3,34},{5,36},{7,38},{9,40},{11,42},{13,44},{15,46},{17,48}... | collective-permute-start | bytes 49160 | tf_op jit(solution)/shard_map/ppermute | solution.py:708
  28.0 16.9 %all-to-all-start = ((f32[32,1,128]{2,1,0:T(1,128)}), f32[32,1,128]{2,1,0:T(1,128)S(1)}, u32[]{:S(2)}, u32[]{:S(2)}) async-start(f32[32,1,128]{2,1,0:T(1,128)} %bitcast.7), calls=%async_computation | async-start | bytes 32768 | tf_op jit(solution)/shard_map/all_to_all | solution.py:733
  35.5 1.3 %collective-permute-start.4 = (f32[8,256]{1,0:T(8,128)S(1)}, f32[8,256]{1,0:T(8,128)S(1)}, u32[]{:S(2)}, u32[]{:S(2)}) collective-permute-start(f32[8,256]{1,0:T(8,128)S(1)} %get-tuple-element.46), channel_id=1, source_target_pairs={{0,1},{1,0},{2,3},{3,2},{4,5},{5,4},{6,7},{7,6},{8,9},{9,8},{10,11... | collective-permute-start | bytes 24584 | tf_op jit(solution)/shard_map/ppermute | solution.py:732

commit v5 on v4

--- a/solution.py
+++ b/solution.py
@@ -214,7 +214,6 @@
 
 def forward_kernel(
     cell_z,
-    side,
     far,
     middle,
     traded,
@@ -236,8 +235,9 @@
     hidden,
     outer,
 ):
-    even = (side[0] & 1) == 0
-    place = side[0] >> 1
+    slab = lax.axis_index("slab")
+    even = (slab & 1) == 0
+    place = ((slab >> 1) + slab + 1) & 1
     outer[place] = far[...]
     outer[1 - place] = traded[...]
 
@@ -503,8 +503,8 @@
     forces[3:8] = jnp.zeros((5, 4 * LAYER), F32)
 
 
-def sums_kernel(parity, middle, forces, along, path, table, kept, sent):
-    even = parity[0] == 0
+def sums_kernel(middle, forces, along, path, table, kept, sent):
+    even = (lax.axis_index("slab") & 1) == 0
     low, high = middle[26:29, :], middle[29:32, :]
     force, beside = forces[0:3], path[0:3]
     up = jnp.where(even, high - low, beside - high)
@@ -523,8 +523,8 @@
     sent[...] = jnp.where(even, right, left)
 
 
-def combine_kernel(images, image_group, parity, climbing, table, own, kept, received, site_of_slot, out, energies):
-    even = parity[0] == 0
+def combine_kernel(images, climbing, table, own, kept, received, site_of_slot, out, energies):
+    even = (lax.axis_index("slab") & 1) == 0
     total = table[0:8]
     for k in range(8, table.shape[0], 8):
         total = total + table[k : k + 8]
@@ -540,7 +540,7 @@
     )
     slot = site_of_slot[...]
     for k, (force, up, down) in enumerate(sides):
-        image = 2 * image_group[0] + k
+        image = 2 * lax.axis_index("image") + k
         here = total[k : k + 1]
         v_prev, v_here, v_next = energy[k : k + 3]
         big = jnp.maximum(jnp.abs(v_next - v_here), jnp.abs(v_prev - v_here))
@@ -601,11 +601,9 @@
 ):
     slabs = lax.axis_size("slab")
     groups = lax.axis_size("image")
-    group = lax.axis_index("image")
     slab = lax.axis_index("slab")
     parity = slab % 2
     even = parity == 0
-    parity_arg = parity.astype(I32).reshape(1)
 
     small = pltpu.CompilerParams(vmem_limit_bytes=4 * 1024 * 1024)
     prepared, site_of_slot = pl.pallas_call(
@@ -636,8 +634,6 @@
         other = p ^ 1 if i % 2 == 0 else (p + 1 if p % 2 else p - 1) % pairs
         partners.append((i, 2 * other + i % 2))
     far = lax.ppermute(middle, "slab", partners)
-    side = ((slab & 1) | ((((slab >> 1) + slab + 1) & 1) << 1)).astype(I32).reshape(1)
-
     def whole(*extents):
         return jax.ShapeDtypeStruct(extents, F32)
 
@@ -678,7 +674,7 @@
             whole(10, 32 * NB, LAYER),
             whole(8, CH, LAYER),
         ),
-        in_specs=[smem()] + [vmem()] * 7,
+        in_specs=[vmem()] * 7,
         out_specs=tuple(vmem() for _ in range(9)),
         scratch_shapes=[
             pltpu.VMEM((12, 8, LAYER), F32),
@@ -688,7 +684,6 @@
         ],
         compiler_params=pltpu.CompilerParams(vmem_limit_bytes=20 * 1024 * 1024),
     )(
-        side,
         far,
         middle,
         traded,
@@ -724,10 +719,10 @@
     table, kept, sent = pl.pallas_call(
         sums_kernel,
         out_shape=(whole(slabs, LAYER), whole(8, 2 * LAYER), whole(8, 2 * LAYER)),
-        in_specs=[smem()] + [vmem()] * 4,
+        in_specs=[vmem()] * 4,
         out_specs=(vmem(), vmem(), vmem()),
         compiler_params=small,
-    )(parity_arg, middle, forces, along, path)
+    )(middle, forces, along, path)
 
     received = lax.ppermute(sent, "slab", [(i, i ^ 1) for i in range(slabs)])
     table = lax.all_to_all(table.reshape(slabs, 1, LAYER), "slab", 0, 0, tiled=False).reshape(slabs, LAYER)
@@ -738,12 +733,10 @@
             jax.ShapeDtypeStruct((3, 2, 2 * LAYER), F32),
             jax.ShapeDtypeStruct((2,), F32),
         ),
-        in_specs=[smem()] * 3 + [vmem()] * 5,
+        in_specs=[smem()] + [vmem()] * 5,
         out_specs=(vmem(), smem()),
         compiler_params=small,
     )(
-        group.astype(I32).reshape(1),
-        parity_arg,
         climbing,
         table,
         prepared,

time: 46.1 us -> 45.4 us (0.985)
  Pallas kernels: 13.8 us -> 13.1 us
where the time goes in v5:
time: 45.4 us; the launch traced here: 45.1 us
  starting transfers between devices  19.8 us (44%)
  Pallas kernels  13.1 us (29%)
  waiting for transfers between devices  10.8 us (24%)
  between operations  1.34 us (3%)
    all_to_all x1, waiting for transfers between devices, local(): lax.all_to_all(table.reshape(slabs, 1, LAYER), 'slab', 0, 0, tiled=False)  8.09 us
    all_to_all x1, starting transfers between devices, local(): lax.all_to_all(table.reshape(slabs, 1, LAYER), 'slab', 0, 0, tiled=False)  7.5 us
    ppermute x1, starting transfers between devices, local(): far = lax.ppermute(middle, 'slab', partners)  6.39 us
    pallas_call x1, Pallas kernels, local(): pl.pallas_call(lambda *refs: forward_kernel(slabs * NZL * LATTICE, *refs)...  5.08 us
    pallas_call x1, Pallas kernels, local(): pl.pallas_call(backward_kernel, out_shape=whole(8, 4 * LAYER), in_specs=[...  3.88 us
    ppermute x1, starting transfers between devices, local(): mate = lax.ppermute(prepared, 'slab', [(i, i ^ 1) for i in range(slabs)])  3.33 us
    ppermute x1, starting transfers between devices, local(): path = lax.ppermute(along, ('image', 'slab'), hops)  2.27 us
    pallas_call x1, Pallas kernels, local(): pl.pallas_call(weights_kernel, out_shape=(jax.ShapeDtypeStruct((4, 2 * CH...  1.34 us
  transfers between devices with their start and end apart: 6, of which 5 were waited for; matrix products, arithmetic and copies ran while one was open for 0% of the time, Pallas kernels for 12%

profile of v5, /device:TPU:1, one launch (start us, length us, event | category | flops | bytes accessed | tf_op | source)
XLA Modules:
  0.0 45.1 jit_solution(12456441433476744803)
XLA Ops:
  0.6 1.2 %shard_map.122 = (f32[32,256]{1,0:T(8,128)S(1)}, s32[8,256]{1,0:T(8,128)S(1)}) custom-call(s32[64,128]{1,0:T(8,128)} %bitcast.9, s32[2,128]{1,0:T(2,128)} %ghost_hbm.1, f32[3,2,256]{2,1,0:T(2,128)} %bitcast.10), custom_call_target="tpu_custom_call" | custom-call | tf_op jit(solution)/shard_map/pallas_call | solution.py:609
  1.8 3.3 %collective-permute-start = (f32[32,256]{1,0:T(8,128)S(1)}, f32[32,256]{1,0:T(8,128)S(1)}, u32[]{:S(2)}, u32[]{:S(2)}) collective-permute-start(f32[32,256]{1,0:T(8,128)S(1)} %get-tuple-element.26.refs_2_), channel_id=1, source_target_pairs={{0,1},{1,0},{2,3},{3,2},{4,5},{5,4},{6,7},{7,6},{8,9},{9,8},{10,11... | collective-permute-start | bytes 98312 | tf_op jit(solution)/shard_map/ppermute | solution.py:628
  5.2 0.9 %collective-permute-done = f32[32,256]{1,0:T(8,128)S(1)} collective-permute-done((f32[32,256]{1,0:T(8,128)S(1)}, f32[32,256]{1,0:T(8,128)S(1)}, u32[]{:S(2)}, u32[]{:S(2)}) %collective-permute-start) | collective-permute-done | bytes 32800 | tf_op jit(solution)/shard_map/ppermute | solution.py:628
  6.0 6.4 %collective-permute-start.1 = (f32[32,512]{1,0:T(8,128)S(1)}, f32[32,512]{1,0:T(8,128)S(1)}, u32[]{:S(2)}, u32[]{:S(2)}) collective-permute-start(f32[32,512]{1,0:T(8,128)S(1)} %pad_maximum_fusion.refs_1_.middle), channel_id=1, source_target_pairs={{0,2},{1,31},{2,0},{3,5},{4,6},{5,3},{6,4},{7,9},{8,10},{9,7},{10,... | collective-permute-start | bytes 196616 | tf_op jit(solution)/shard_map/ppermute | solution.py:636
  12.4 1.3 %shard_map.123 = (bf16[4,256,256]{2,1,0:T(8,128)(2,1)S(1)}, bf16[4,256,256]{2,1,0:T(8,128)(2,1)S(1)}, bf16[2,16,256]{2,1,0:T(8,128)(2,1)S(1)}, bf16[2,128,32]{2,1,0:T(8,128)(2,1)S(1)}, f32[128,128]{1,0:T(8,128)S(1)}) custom-call(f32[128,128]{1,0:T(8,128)} %w_square.1, f32[128,128]{1,0:T(8,128)} %w_hidden.1, f32[128,128]{1,0:T(8,128)} %w_message.1, ...), custom_call_target="tpu_custom_call" | custom-call | flops 100000000 | bytes 4194304 | tf_op jit(solution)/shard_map/pallas_call | solution.py:640
  13.8 0.3 collective-permute-done.1.refs_0_
  14.1 0.0 collective-permute-start.2
  14.1 1.3 %collective-permute-done.2.refs_2_ = f32[32,512]{1,0:T(8,128)S(1)} collective-permute-done((f32[32,512]{1,0:T(8,128)S(1)}, f32[32,512]{1,0:T(8,128)S(1)}, u32[]{:S(2)}, u32[]{:S(2)}) %collective-permute-start.2) | collective-permute-done | bytes 65568 | tf_op jit(solution)/shard_map/ppermute | solution.py:662
  15.3 5.1 %shard_map.124 = (f32[8,512]{1,0:T(8,128)S(1)}, f32[4,3,32,128]{3,2,1,0:T(8,128)S(1)}, f32[4,32,128]{2,1,0:T(8,128)S(1)}, f32[6,256,128]{2,1,0:T(8,128)S(1)}, f3...) custom-call(f32[32,512]{1,0:T(8,128)S(1)} %collective-permute-done.1, ...), custom_call_target="tpu_custom_call" | custom-call | tf_op jit(solution)/shard_map/pallas_call | solution.py:664
  20.4 2.3 %collective-permute-start.3 = (f32[8,512]{1,0:T(8,128)S(1)}, f32[8,512]{1,0:T(8,128)S(1)}, u32[]{:S(2)}, u32[]{:S(2)}) collective-permute-start(f32[8,512]{1,0:T(8,128)S(1)} %get-tuple-element.43.along), channel_id=1, source_target_pairs={{1,32},{3,34},{5,36},{7,38},{9,40},{11,42},{13,44},{15,46},{17,48}... | collective-permute-start | bytes 49160 | tf_op jit(solution)/shard_map/ppermute | solution.py:703
  22.7 3.9 %shard_map.125.forces = f32[8,512]{1,0:T(8,128)S(1)} custom-call(f32[4,3,32,128]{3,2,1,0:T(8,128)S(1)} %get-tuple-element.34.reach, f32[4,32,128]{2,1,0:T(8,128)S(1)} %get-tuple-element.35.inverse_radius, f32[6,256,128]{2,1,0:T(8,128)S(1)} %get-tuple-element.36.slope, f32[6,128,128]{2,1,0:T(8,128)S(1)} %get-tuple-element.37.radial_mix, ...), custom_call_target="tpu_custom_call" | custom-call | flops 4000000000 | bytes 4194304 | tf_op jit(solution)/shard_map/pallas_call | solution.py:705
  26.6 0.0 collective-permute-done.3.path
  26.6 0.7 %shard_map.126 = (f32[32,128]{1,0:T(8,128)}, f32[8,256]{1,0:T(8,128)S(1)}, f32[8,256]{1,0:T(8,128)S(1)}) custom-call(f32[32,512]{1,0:T(8,128)S(1)} %pad_maximum_fusion.refs_1_.middle, f32[8,512]{1,0:T(8,128)S(1)} %shard_map.125.forces, f32[8,512]{1,0:T(8,128)S(1)} %get-tuple-element.43.along, f32[8,512]{1,0:T(8,128)S(1)} %collective-permute-done.3.path), custom_call_target="tpu_custom_call" | custom-call | tf_op jit(solution)/shard_map/pallas_call | solution.py:719
  27.3 7.5 %all-to-all-start = ((f32[32,1,128]{2,1,0:T(1,128)}), f32[32,1,128]{2,1,0:T(1,128)S(1)}, u32[]{:S(2)}, u32[]{:S(2)}) async-start(f32[32,1,128]{2,1,0:T(1,128)} %bitcast.4), calls=%async_computation | async-start | bytes 32768 | tf_op jit(solution)/shard_map/all_to_all | solution.py:728
  34.8 0.3 collective-permute-start.4
  35.8 0.3 collective-permute-done.4.refs_4_
  36.1 8.1 %all-to-all-done = f32[32,1,128]{2,1,0:T(1,128)S(1)} async-done(((f32[32,1,128]{2,1,0:T(1,128)}), f32[32,1,128]{2,1,0:T(1,128)S(1)}, u32[]{:S(2)}, u32[]{:S(2)}) %all-to-all-start) | async-done | bytes 16416 | tf_op jit(solution)/shard_map/all_to_all | solution.py:728
  44.2 0.9 %shard_map.127 = (f32[3,2,256]{2,1,0:T(2,128)}, f32[2]{0:T(128)}) custom-call(s32[1]{0:T(128)S(6)} %copy.14.refs_0_, f32[32,128]{1,0:T(8,128)S(1)} %bitcast.8, f32[32,256]{1,0:T(8,128)S(1)} %get-tuple-element.26.refs_2_, f32[8,256]{1,0:T(8,128)S(1)} %get-tuple-element.45.refs_3_, f32[8,256]{1,0:T(8,128)S(1)} %collective-permute-done.4.refs_4_, ...), custom_call_target="tpu_custom_call" | custom-call | tf_op jit(solution)/shard_map/pallas_call | solution.py:730
  (2 shorter events, 0.0 us)
Async XLA Ops:
  1.8 4.2 %collective-permute-start = (f32[32,256]{1,0:T(8,128)S(1)}, f32[32,256]{1,0:T(8,128)S(1)}, u32[]{:S(2)}, u32[]{:S(2)}) collective-permute-start(f32[32,256]{1,0:T(8,128)S(1)} %get-tuple-element.26.refs_2_), channel_id=1, source_target_pairs={{0,1},{1,0},{2,3},{3,2},{4,5},{5,4},{6,7},{7,6},{8,9},{9,8},{10,11... | collective-permute-start | bytes 98312 | tf_op jit(solution)/shard_map/ppermute | solution.py:628
  6.0 8.0 %collective-permute-start.1 = (f32[32,512]{1,0:T(8,128)S(1)}, f32[32,512]{1,0:T(8,128)S(1)}, u32[]{:S(2)}, u32[]{:S(2)}) collective-permute-start(f32[32,512]{1,0:T(8,128)S(1)} %pad_maximum_fusion.refs_1_.middle), channel_id=1, source_target_pairs={{0,2},{1,31},{2,0},{3,5},{4,6},{5,3},{6,4},{7,9},{8,10},{9,7},{10,... | collective-permute-start | bytes 196616 | tf_op jit(solution)/shard_map/ppermute | solution.py:636
  14.1 1.3 %collective-permute-start.2 = (f32[32,512]{1,0:T(8,128)S(1)}, f32[32,512]{1,0:T(8,128)S(1)}, u32[]{:S(2)}, u32[]{:S(2)}) collective-permute-start(f32[32,512]{1,0:T(8,128)S(1)} %collective-permute-done.1.refs_0_), channel_id=1, source_target_pairs={{0,1},{1,0},{2,3},{3,2},{4,5},{5,4},{6,7},{7,6},{8,9},{9,8},{10,11... | collective-permute-start | bytes 196616 | tf_op jit(solution)/shard_map/ppermute | solution.py:662
  20.4 6.2 %collective-permute-start.3 = (f32[8,512]{1,0:T(8,128)S(1)}, f32[8,512]{1,0:T(8,128)S(1)}, u32[]{:S(2)}, u32[]{:S(2)}) collective-permute-start(f32[8,512]{1,0:T(8,128)S(1)} %get-tuple-element.43.along), channel_id=1, source_target_pairs={{1,32},{3,34},{5,36},{7,38},{9,40},{11,42},{13,44},{15,46},{17,48}... | collective-permute-start | bytes 49160 | tf_op jit(solution)/shard_map/ppermute | solution.py:703
  27.3 16.9 %all-to-all-start = ((f32[32,1,128]{2,1,0:T(1,128)}), f32[32,1,128]{2,1,0:T(1,128)S(1)}, u32[]{:S(2)}, u32[]{:S(2)}) async-start(f32[32,1,128]{2,1,0:T(1,128)} %bitcast.4), calls=%async_computation | async-start | bytes 32768 | tf_op jit(solution)/shard_map/all_to_all | solution.py:728
  34.8 1.3 %collective-permute-start.4 = (f32[8,256]{1,0:T(8,128)S(1)}, f32[8,256]{1,0:T(8,128)S(1)}, u32[]{:S(2)}, u32[]{:S(2)}) collective-permute-start(f32[8,256]{1,0:T(8,128)S(1)} %get-tuple-element.46), channel_id=1, source_target_pairs={{0,1},{1,0},{2,3},{3,2},{4,5},{5,4},{6,7},{7,6},{8,9},{9,8},{10,11... | collective-permute-start | bytes 24584 | tf_op jit(solution)/shard_map/ppermute | solution.py:727

commit v6 on v5

--- a/solution.py
+++ b/solution.py
@@ -105,8 +105,7 @@
     ]
     for copy in copies:
         copy.start()
-    for copy in copies:
-        copy.wait()
+    copies[0].wait()
     slots = ghost_slots[...]
     inverse = jnp.zeros((8, 2 * LAYER), F32)
     for layer in range(NZL):
@@ -122,6 +121,8 @@
     site_of_slot[...] = inverse
     first = jnp.broadcast_to(inverse[0:1, :LAYER], (32, LAYER))
     second = jnp.broadcast_to(inverse[0:1, LAYER:], (32, LAYER))
+    copies[1].wait()
+    copies[2].wait()
     sides = [
         jnp.concatenate(
             [positions[c, k : k + 1, half * LAYER : (half + 1) * LAYER] for k in range(2) for c in range(3)]

time: 45.4 us -> 45.4 us (level)
  no operation moved by 1% of the time
where the time goes in v6:
time: 45.4 us; the launch traced here: 45.2 us
  starting transfers between devices  19.8 us (44%)
  Pallas kernels  13.2 us (29%)
  waiting for transfers between devices  10.8 us (24%)
  between operations  1.34 us (3%)
    all_to_all x1, waiting for transfers between devices, local(): lax.all_to_all(table.reshape(slabs, 1, LAYER), 'slab', 0, 0, tiled=False)  8.09 us
    all_to_all x1, starting transfers between devices, local(): lax.all_to_all(table.reshape(slabs, 1, LAYER), 'slab', 0, 0, tiled=False)  7.5 us
    ppermute x1, starting transfers between devices, local(): far = lax.ppermute(middle, 'slab', partners)  6.39 us
    pallas_call x1, Pallas kernels, local(): pl.pallas_call(lambda *refs: forward_kernel(slabs * NZL * LATTICE, *refs)...  5.08 us
    pallas_call x1, Pallas kernels, local(): pl.pallas_call(backward_kernel, out_shape=whole(8, 4 * LAYER), in_specs=[...  3.88 us
    ppermute x1, starting transfers between devices, local(): mate = lax.ppermute(prepared, 'slab', [(i, i ^ 1) for i in range(slabs)])  3.33 us
    ppermute x1, starting transfers between devices, local(): path = lax.ppermute(along, ('image', 'slab'), hops)  2.26 us
    pallas_call x1, Pallas kernels, local(): pl.pallas_call(weights_kernel, out_shape=(jax.ShapeDtypeStruct((4, 2 * CH...  1.34 us
  transfers between devices with their start and end apart: 6, of which 5 were waited for; matrix products, arithmetic and copies ran while one was open for 0% of the time, Pallas kernels for 12%

profile of v6, /device:TPU:1, one launch (start us, length us, event | category | flops | bytes accessed | tf_op | source)
XLA Modules:
  0.0 45.2 jit_solution(9089688773025098688)
XLA Ops:
  0.6 1.2 %shard_map.122 = (f32[32,256]{1,0:T(8,128)S(1)}, s32[8,256]{1,0:T(8,128)S(1)}) custom-call(s32[64,128]{1,0:T(8,128)} %bitcast.9, s32[2,128]{1,0:T(2,128)} %ghost_hbm.1, f32[3,2,256]{2,1,0:T(2,128)} %bitcast.10), custom_call_target="tpu_custom_call" | custom-call | tf_op jit(solution)/shard_map/pallas_call | solution.py:610
  1.9 3.3 %collective-permute-start = (f32[32,256]{1,0:T(8,128)S(1)}, f32[32,256]{1,0:T(8,128)S(1)}, u32[]{:S(2)}, u32[]{:S(2)}) collective-permute-start(f32[32,256]{1,0:T(8,128)S(1)} %get-tuple-element.26.refs_2_), channel_id=1, source_target_pairs={{0,1},{1,0},{2,3},{3,2},{4,5},{5,4},{6,7},{7,6},{8,9},{9,8},{10,11... | collective-permute-start | bytes 98312 | tf_op jit(solution)/shard_map/ppermute | solution.py:629
  5.2 0.9 %collective-permute-done = f32[32,256]{1,0:T(8,128)S(1)} collective-permute-done((f32[32,256]{1,0:T(8,128)S(1)}, f32[32,256]{1,0:T(8,128)S(1)}, u32[]{:S(2)}, u32[]{:S(2)}) %collective-permute-start) | collective-permute-done | bytes 32800 | tf_op jit(solution)/shard_map/ppermute | solution.py:629
  6.1 6.4 %collective-permute-start.1 = (f32[32,512]{1,0:T(8,128)S(1)}, f32[32,512]{1,0:T(8,128)S(1)}, u32[]{:S(2)}, u32[]{:S(2)}) collective-permute-start(f32[32,512]{1,0:T(8,128)S(1)} %pad_maximum_fusion.refs_1_.middle), channel_id=1, source_target_pairs={{0,2},{1,31},{2,0},{3,5},{4,6},{5,3},{6,4},{7,9},{8,10},{9,7},{10,... | collective-permute-start | bytes 196616 | tf_op jit(solution)/shard_map/ppermute | solution.py:637
  12.5 1.3 %shard_map.123 = (bf16[4,256,256]{2,1,0:T(8,128)(2,1)S(1)}, bf16[4,256,256]{2,1,0:T(8,128)(2,1)S(1)}, bf16[2,16,256]{2,1,0:T(8,128)(2,1)S(1)}, bf16[2,128,32]{2,1,0:T(8,128)(2,1)S(1)}, f32[128,128]{1,0:T(8,128)S(1)}) custom-call(f32[128,128]{1,0:T(8,128)} %w_square.1, f32[128,128]{1,0:T(8,128)} %w_hidden.1, f32[128,128]{1,0:T(8,128)} %w_message.1, ...), custom_call_target="tpu_custom_call" | custom-call | flops 100000000 | bytes 4194304 | tf_op jit(solution)/shard_map/pallas_call | solution.py:641
  13.8 0.3 collective-permute-done.1.refs_0_
  14.1 0.0 collective-permute-start.2
  14.1 1.3 %collective-permute-done.2.refs_2_ = f32[32,512]{1,0:T(8,128)S(1)} collective-permute-done((f32[32,512]{1,0:T(8,128)S(1)}, f32[32,512]{1,0:T(8,128)S(1)}, u32[]{:S(2)}, u32[]{:S(2)}) %collective-permute-start.2) | collective-permute-done | bytes 65568 | tf_op jit(solution)/shard_map/ppermute | solution.py:663
  15.4 5.1 %shard_map.124 = (f32[8,512]{1,0:T(8,128)S(1)}, f32[4,3,32,128]{3,2,1,0:T(8,128)S(1)}, f32[4,32,128]{2,1,0:T(8,128)S(1)}, f32[6,256,128]{2,1,0:T(8,128)S(1)}, f3...) custom-call(f32[32,512]{1,0:T(8,128)S(1)} %collective-permute-done.1, ...), custom_call_target="tpu_custom_call" | custom-call | tf_op jit(solution)/shard_map/pallas_call | solution.py:665
  20.5 2.3 %collective-permute-start.3 = (f32[8,512]{1,0:T(8,128)S(1)}, f32[8,512]{1,0:T(8,128)S(1)}, u32[]{:S(2)}, u32[]{:S(2)}) collective-permute-start(f32[8,512]{1,0:T(8,128)S(1)} %get-tuple-element.43.along), channel_id=1, source_target_pairs={{1,32},{3,34},{5,36},{7,38},{9,40},{11,42},{13,44},{15,46},{17,48}... | collective-permute-start | bytes 49160 | tf_op jit(solution)/shard_map/ppermute | solution.py:704
  22.7 3.9 %shard_map.125.forces = f32[8,512]{1,0:T(8,128)S(1)} custom-call(f32[4,3,32,128]{3,2,1,0:T(8,128)S(1)} %get-tuple-element.34.reach, f32[4,32,128]{2,1,0:T(8,128)S(1)} %get-tuple-element.35.inverse_radius, f32[6,256,128]{2,1,0:T(8,128)S(1)} %get-tuple-element.36.slope, f32[6,128,128]{2,1,0:T(8,128)S(1)} %get-tuple-element.37.radial_mix, ...), custom_call_target="tpu_custom_call" | custom-call | flops 4000000000 | bytes 4194304 | tf_op jit(solution)/shard_map/pallas_call | solution.py:706
  26.6 0.0 collective-permute-done.3.path
  26.6 0.7 %shard_map.126 = (f32[32,128]{1,0:T(8,128)}, f32[8,256]{1,0:T(8,128)S(1)}, f32[8,256]{1,0:T(8,128)S(1)}) custom-call(f32[32,512]{1,0:T(8,128)S(1)} %pad_maximum_fusion.refs_1_.middle, f32[8,512]{1,0:T(8,128)S(1)} %shard_map.125.forces, f32[8,512]{1,0:T(8,128)S(1)} %get-tuple-element.43.along, f32[8,512]{1,0:T(8,128)S(1)} %collective-permute-done.3.path), custom_call_target="tpu_custom_call" | custom-call | tf_op jit(solution)/shard_map/pallas_call | solution.py:720
  27.4 7.5 %all-to-all-start = ((f32[32,1,128]{2,1,0:T(1,128)}), f32[32,1,128]{2,1,0:T(1,128)S(1)}, u32[]{:S(2)}, u32[]{:S(2)}) async-start(f32[32,1,128]{2,1,0:T(1,128)} %bitcast.4), calls=%async_computation | async-start | bytes 32768 | tf_op jit(solution)/shard_map/all_to_all | solution.py:729
  34.9 0.3 collective-permute-start.4
  35.8 0.3 collective-permute-done.4.refs_4_
  36.1 8.1 %all-to-all-done = f32[32,1,128]{2,1,0:T(1,128)S(1)} async-done(((f32[32,1,128]{2,1,0:T(1,128)}), f32[32,1,128]{2,1,0:T(1,128)S(1)}, u32[]{:S(2)}, u32[]{:S(2)}) %all-to-all-start) | async-done | bytes 16416 | tf_op jit(solution)/shard_map/all_to_all | solution.py:729
  44.2 0.9 %shard_map.127 = (f32[3,2,256]{2,1,0:T(2,128)}, f32[2]{0:T(128)}) custom-call(s32[1]{0:T(128)S(6)} %copy.14.refs_0_, f32[32,128]{1,0:T(8,128)S(1)} %bitcast.8, f32[32,256]{1,0:T(8,128)S(1)} %get-tuple-element.26.refs_2_, f32[8,256]{1,0:T(8,128)S(1)} %get-tuple-element.45.refs_3_, f32[8,256]{1,0:T(8,128)S(1)} %collective-permute-done.4.refs_4_, ...), custom_call_target="tpu_custom_call" | custom-call | tf_op jit(solution)/shard_map/pallas_call | solution.py:731
  (2 shorter events, 0.0 us)
Async XLA Ops:
  1.9 4.2 %collective-permute-start = (f32[32,256]{1,0:T(8,128)S(1)}, f32[32,256]{1,0:T(8,128)S(1)}, u32[]{:S(2)}, u32[]{:S(2)}) collective-permute-start(f32[32,256]{1,0:T(8,128)S(1)} %get-tuple-element.26.refs_2_), channel_id=1, source_target_pairs={{0,1},{1,0},{2,3},{3,2},{4,5},{5,4},{6,7},{7,6},{8,9},{9,8},{10,11... | collective-permute-start | bytes 98312 | tf_op jit(solution)/shard_map/ppermute | solution.py:629
  6.1 8.0 %collective-permute-start.1 = (f32[32,512]{1,0:T(8,128)S(1)}, f32[32,512]{1,0:T(8,128)S(1)}, u32[]{:S(2)}, u32[]{:S(2)}) collective-permute-start(f32[32,512]{1,0:T(8,128)S(1)} %pad_maximum_fusion.refs_1_.middle), channel_id=1, source_target_pairs={{0,2},{1,31},{2,0},{3,5},{4,6},{5,3},{6,4},{7,9},{8,10},{9,7},{10,... | collective-permute-start | bytes 196616 | tf_op jit(solution)/shard_map/ppermute | solution.py:637
  14.1 1.3 %collective-permute-start.2 = (f32[32,512]{1,0:T(8,128)S(1)}, f32[32,512]{1,0:T(8,128)S(1)}, u32[]{:S(2)}, u32[]{:S(2)}) collective-permute-start(f32[32,512]{1,0:T(8,128)S(1)} %collective-permute-done.1.refs_0_), channel_id=1, source_target_pairs={{0,1},{1,0},{2,3},{3,2},{4,5},{5,4},{6,7},{7,6},{8,9},{9,8},{10,11... | collective-permute-start | bytes 196616 | tf_op jit(solution)/shard_map/ppermute | solution.py:663
  20.5 6.2 %collective-permute-start.3 = (f32[8,512]{1,0:T(8,128)S(1)}, f32[8,512]{1,0:T(8,128)S(1)}, u32[]{:S(2)}, u32[]{:S(2)}) collective-permute-start(f32[8,512]{1,0:T(8,128)S(1)} %get-tuple-element.43.along), channel_id=1, source_target_pairs={{1,32},{3,34},{5,36},{7,38},{9,40},{11,42},{13,44},{15,46},{17,48}... | collective-permute-start | bytes 49160 | tf_op jit(solution)/shard_map/ppermute | solution.py:704
  27.4 16.9 %all-to-all-start = ((f32[32,1,128]{2,1,0:T(1,128)}), f32[32,1,128]{2,1,0:T(1,128)S(1)}, u32[]{:S(2)}, u32[]{:S(2)}) async-start(f32[32,1,128]{2,1,0:T(1,128)} %bitcast.4), calls=%async_computation | async-start | bytes 32768 | tf_op jit(solution)/shard_map/all_to_all | solution.py:729
  34.9 1.3 %collective-permute-start.4 = (f32[8,256]{1,0:T(8,128)S(1)}, f32[8,256]{1,0:T(8,128)S(1)}, u32[]{:S(2)}, u32[]{:S(2)}) collective-permute-start(f32[8,256]{1,0:T(8,128)S(1)} %get-tuple-element.46), channel_id=1, source_target_pairs={{0,1},{1,0},{2,3},{3,2},{4,5},{5,4},{6,7},{7,6},{8,9},{9,8},{10,11... | collective-permute-start | bytes 24584 | tf_op jit(solution)/shard_map/ppermute | solution.py:728
